TPU v7x, 128 devices: a whole 4x4x4 slice. The times are simulated.
128 devices in a mesh: pair: 16 (over x, z), virt: 8 (over y, core).
Axes of the slice: x: 4, y: 4, z: 4, core: 2. Of those that a mesh axis runs over, the one named last changes fastest.
Arguments:
- lambda_blocks: float32 [32, 1920, 1920], P('pair', 'virt'), may hold values from -1 to 1
- amplitudes: float32 [32, 1920, 1920], P('pair', 'virt'), may hold values from -1 to 1
- pair_list: int32 [32, 2], replicated, may hold values from 0 to 199, as said below
Outputs:
- density_virt: float32 [1920, 1920], P('virt', 'pair')
- density_occ: float32 [200, 200], replicated
Inputs may be any that keep to these rules, and one draw needn't show every extreme that they name: `pair_list`: column 0 holds an occupied index below 200, reaching 199; column 1 holds one below 8; pairs may repeat.
All inputs are finite; a program needn't handle non-finite values.
Results may differ from a plain program's by a relative error of at most 0.00013.
Values sent between devices are 32-bit elements; how exact they have to be, the bound alone decides.
A program may use at most 256 MiB of HBM per device.

v0:
```python
import jax
import jax.numpy as jnp
from jax import lax
from jax.sharding import PartitionSpec as P

OCC = 200


def shards(lambda_blocks, amplitudes, pair_list):
    highest = lax.Precision.HIGHEST
    partial_rows = jnp.einsum(
        "pac,pbc->ab",
        lambda_blocks,
        lax.all_gather(amplitudes, "virt", axis=1, tiled=True),
        precision=highest,
    )
    density_virt = lax.psum_scatter(partial_rows, "pair", scatter_dimension=1, tiled=True)
    all_lambda, all_amps = (
        lax.all_to_all(lambda_blocks, "pair", split_axis=2, concat_axis=0, tiled=True),
        lax.all_to_all(amplitudes, "pair", split_axis=2, concat_axis=0, tiled=True),
    )
    intersection_part = jnp.einsum("pac,qac->pq", all_lambda, all_amps, precision=highest)
    intersection = lax.psum(intersection_part, ("pair", "virt"))
    first = pair_list[:, 0]
    second = pair_list[:, 1]
    one_hot = (first[:, None] == jnp.arange(OCC, dtype=jnp.int32)[None, :]).astype(jnp.float32)
    same_k = (second[:, None] == second[None, :]).astype(jnp.float32)
    inner = jnp.dot(same_k * intersection, one_hot, precision=highest)
    density_occ = -jnp.dot(one_hot.T, inner, precision=highest)
    return (density_virt, density_occ)


def solution(mesh):
    in_specs = (P("pair", "virt", None), P("pair", "virt", None), P())
    out_specs = (P("virt", "pair"), P())
    return jax.shard_map(shards, mesh=mesh, in_specs=in_specs, out_specs=out_specs, check_vma=False)
```

profile of v0, /device:TPU:16, one launch (start us, length us, event | category | flops | bytes accessed | tf_op | source)
XLA Modules:
  0.0 281.0 jit_solution(12196437769663713546)
XLA Ops:
  7.2 0.0 all-gather.2.cloned.1.call-start
  7.2 0.7 all-gather.2.cloned.1.call-update
  7.9 7.0 %copy.12 = f32[2,240,1920]{1,0,2:T(2,128)} copy(f32[2,240,1920]{2,1,0:T(8,128)} %param.4) | data formatting | bytes 7372800 | tf_op args[1]
  14.9 7.9 %all-to-all-start.1 = ((f32[2,240,1920]{1,0,2:T(2,128)}), f32[2,240,1920]{1,0,2:T(2,128)}, u32[]{:S(2)}, u32[]{:S(2)}) async-start(f32[2,240,1920]{1,0,2:T(2,128)} %copy.12), calls=%async_computation.1 | async-start | bytes 7864320 | tf_op jit(solution)/shard_map/all_to_all | solution.py:20
  22.8 7.5 %copy.9 = f32[2,240,1920]{1,0,2:T(2,128)} copy(f32[2,240,1920]{2,1,0:T(8,128)} %param.3) | data formatting | bytes 7372800 | tf_op args[0]
  30.3 50.0 %all-to-all-done.1 = f32[2,240,1920]{1,0,2:T(2,128)} async-done(((f32[2,240,1920]{1,0,2:T(2,128)}), f32[2,240,1920]{1,0,2:T(2,128)}, u32[]{:S(2)}, u32[]{:S(2)}) %all-to-all-start.1) | async-done | bytes 3686432 | tf_op jit(solution)/shard_map/all_to_all | solution.py:20
  80.3 10.5 %all-to-all-start = ((f32[2,240,1920]{1,0,2:T(2,128)}), f32[2,240,1920]{1,0,2:T(2,128)}, u32[]{:S(2)}, u32[]{:S(2)}) async-start(f32[2,240,1920]{1,0,2:T(2,128)} %copy.9), calls=%async_computation | async-start | bytes 7864320 | tf_op jit(solution)/shard_map/all_to_all | solution.py:19
  90.8 0.0 copy-start.1
  90.8 0.0 copy-start
  90.8 0.0 all-reduce.3.cloned.1.call-start
  90.9 59.4 %all-gather.2.cloned.1.call-done = f32[2,1920,1920]{2,1,0:T(8,128)} async-done(((f32[2,240,1920]{2,1,0:T(8,128)}), f32[2,1920,1920]{2,1,0:T(8,128)}) %all-gather.2.cloned.1.call-update) | async-done | bytes 29491216 | tf_op jit(solution)/shard_map/all_gather | solution.py:14
  150.3 30.7 %convolution_bitcast_fusion = f32[240,1920]{1,0:T(8,128)} fusion(f32[2,240,1920]{2,1,0:T(8,128)} %param.3, f32[2,1920,1920]{2,1,0:T(8,128)} %all-gather.2.cloned.1.call-done), kind=kOutput, calls=%fused_computation.3 | convolution fusion | flops 21233664000 | bytes 35020800 | tf_op jit(solution)/shard_map/pac,pbc->ab/dot_general | solution.py:11
  181.0 0.0 all-reduce.3.cloned.1.call-update
  181.0 0.0 copy-done.1
  181.0 0.6 dynamic-slice
  182.3 0.0 copy-done
  182.3 7.1 %copy.20 = f32[2,240,16,120]{3,1,0,2:T(8,128)} copy(f32[2,240,16,120]{1,0,3,2:T(2,128)} %bitcast.7) | data formatting | bytes 7372800 | tf_op jit(solution)/shard_map/all_to_all | solution.py:20
  189.4 0.0 all-to-all-done
  189.4 7.1 %copy.18 = f32[2,240,16,120]{3,1,0,2:T(8,128)} copy(f32[2,240,16,120]{1,0,3,2:T(2,128)} %bitcast.3) | data formatting | bytes 7372800 | tf_op jit(solution)/shard_map/all_to_all | solution.py:19
  196.5 8.9 %fusion.3 = f32[32,32]{1,0:T(8,128)S(1)} fusion(f32[32,240,120]{2,1,0:T(8,128)} %bitcast.24, f32[32,240,120]{2,1,0:T(8,128)} %bitcast.25), kind=kOutput, calls=%fused_computation.5 | convolution fusion | flops 353894400 | bytes 7376896 | tf_op jit(solution)/shard_map/pac,qac->pq/dot_general | solution.py:22
  205.3 65.9 %psum.7 = f32[32,32]{1,0:T(8,128)S(1)} all-reduce(f32[32,32]{1,0:T(8,128)S(1)} %fusion.3), channel_id=1, replica_groups=mesh['pair'=16,'virt'=8] {'pair','virt'}, use_global_device_ids=true, to_apply=%region_1.0 | all-reduce | flops 1024 | bytes 8192 | tf_op jit(solution)/shard_map/psum | solution.py:23
  271.2 0.2 fusion.8
  271.4 1.0 convolution_negate_fusion
  272.5 0.0 all-reduce.3.cloned.1.call-done
  272.5 1.7 constant_dynamic-slice_fusion
  (1 shorter events, 0.0 us)
Async XLA Ops:
  7.2 143.1 %all-gather.2.cloned.1.call-start = ((), (), s32[]{:S(2)}) async-start(), calls=%async_computation.2 | async-start | bytes 33177600 | tf_op jit(solution)/shard_map/all_gather | solution.py:14
  14.9 65.4 %all-to-all-start.1 = ((f32[2,240,1920]{1,0,2:T(2,128)}), f32[2,240,1920]{1,0,2:T(2,128)}, u32[]{:S(2)}, u32[]{:S(2)}) async-start(f32[2,240,1920]{1,0,2:T(2,128)} %copy.12), calls=%async_computation.1 | async-start | bytes 7864320 | tf_op jit(solution)/shard_map/all_to_all | solution.py:20
  80.3 109.1 %all-to-all-start = ((f32[2,240,1920]{1,0,2:T(2,128)}), f32[2,240,1920]{1,0,2:T(2,128)}, u32[]{:S(2)}, u32[]{:S(2)}) async-start(f32[2,240,1920]{1,0,2:T(2,128)} %copy.9), calls=%async_computation | async-start | bytes 7864320 | tf_op jit(solution)/shard_map/all_to_all | solution.py:19
  90.8 90.2 %copy-start.1 = (u32[128]{0:T(128)S(1)}, u32[128]{0:T(128)}, u32[]{:S(2)}) copy-start(u32[128]{0:T(128)} %constant.6) | copy-start | bytes 1540
  90.8 91.5 %copy-start = (s32[32,2]{0,1:T(2,128)S(1)}, s32[32,2]{0,1:T(2,128)}, u32[]{:S(2)}) copy-start(s32[32,2]{0,1:T(2,128)} %param.5) | copy-start | bytes 772
  90.8 181.7 %all-reduce.3.cloned.1.call-start = ((), (), s32[]{:S(2)}) async-start(), calls=%async_computation.3 | async-start | bytes 3686400
Sparse Core Ops, SparseCore 0:
  9.7 140.5 all-gather.1
  181.1 90.4 all-reduce.2
where the time goes:
time: 284 us; the launch traced here: 281 us
  waiting for transfers between devices  110 us (39%)
  blocking collectives  65.9 us (23%)
  matrix products  40.8 us (14%)
  local copies, waits for them, and re-layouts  30.9 us (11%)
  starting transfers between devices  18.5 us (7%)
  between operations  14.8 us (5%)
    psum x1, blocking collectives, shards(): intersection = lax.psum(intersection_part, ('pair', 'virt'))  65.9 us
    all_gather x1, waiting for transfers between devices, shards(): lax.all_gather(amplitudes, 'virt', axis=1, tiled=True)  59.4 us
    all_to_all x1, waiting for transfers between devices, shards(): lax.all_to_all(amplitudes, 'pair', split_axis=2, concat_axis=0, tiled=True)  50 us
    dot_general x1, matrix products, shards(): jnp.einsum('pac,pbc->ab', lambda_blocks, lax.all_gather(amplitudes, 'virt...  30.7 us
    unnamed x8, local copies, waits for them, and re-layouts  16.8 us
    all_to_all x1, starting transfers between devices, shards(): lax.all_to_all(lambda_blocks, 'pair', split_axis=2, concat_axis=0, tiled=...  10.5 us
    dot_general x1, matrix products, shards(): jnp.einsum('pac,qac->pq', all_lambda, all_amps, precision=highest)  8.85 us
    all_to_all x1, starting transfers between devices, shards(): lax.all_to_all(amplitudes, 'pair', split_axis=2, concat_axis=0, tiled=True)  7.92 us
  transfers between devices with their start and end apart: 4, of which 2 were waited for; matrix products, arithmetic and copies ran while one was open for 25% of the time, Pallas kernels for 0%

commit v1 on v0

v1 whole, which is shorter than its diff:
```python
import jax
import jax.numpy as jnp
from jax import lax
from jax.experimental import pallas as pl
from jax.experimental.pallas import tpu as pltpu
from jax.sharding import PartitionSpec as P

OCC = 200
NP = 32
ROWS = 240
PAD = 256
V = 1920
KC = 640
KPARTS = V // KC
STEPS = 2 * KPARTS
MESH = pl.DeviceIdType.MESH
F32 = jnp.float32
BF16 = jnp.bfloat16


class Copy:
    def __init__(self, *variants):
        self.variants = variants

    def _each(self, act):
        for cond, make in self.variants:
            if cond is None:
                act(make())
            else:

                @pl.when(cond)
                def _(make=make):
                    act(make())

    def start(self):
        self._each(lambda c: c.start())

    def wait_send(self):
        self._each(lambda c: c.wait_send())

    def wait_recv(self):
        self._each(lambda c: c.wait_recv())

    def wait(self):
        self._each(lambda c: c.wait())


class Sems:
    def __init__(self, send, recv):
        self.send, self.recv, self.n = send, recv, 0

    def take(self):
        self.n += 1
        return self.send.at[self.n - 1], self.recv.at[self.n - 1]


def split(v):
    hi = v.astype(BF16)
    return hi, (v - hi.astype(F32)).astype(BF16)


NT = (((1,), (1,)), ((), ()))


def dot_nt(a, b):
    return lax.dot_general(a, b, NT, preferred_element_type=F32)


N_SEMS = 128


def kernel(
    l_ref, t_ref, out_ref, inter_ref,
    lraw, traw, lcat, tcat, acc, lx, tz, lz, tx, gram,
    ro1, ro2, rp1, rp2, so, sp, fo, fp, yq, fin, ix, iz, iy, ic,
    send, recv, local,
):
    pair, virt = lax.axis_index("pair"), lax.axis_index("virt")
    x, z = lax.div(pair, 4), lax.rem(pair, 4)
    y, c = lax.div(virt, 2), lax.rem(virt, 2)
    sems = Sems(send, recv)

    def ring(a):
        return lax.rem(a + 4, 4)

    def dev(xx, zz, yy, cc):
        return (xx * 4 + zz, yy * 2 + cc)

    def at_x(d):
        return dev(ring(x + d), z, y, c)

    def at_z(d):
        return dev(x, ring(z + d), y, c)

    def at_y(d):
        return dev(x, z, ring(y + d), c)

    other = dev(x, z, y, 1 - c)
    y_l = y + 1 - 2 * lax.rem(y, 2)
    y_t = 3 - y
    to_l, to_t = dev(x, z, y_l, c), dev(x, z, y_t, c)

    def remote(src, dst, device, pair_of_sems):
        s, r = pair_of_sems
        return Copy((None, lambda: pltpu.make_async_remote_copy(src_ref=src(), dst_ref=dst(), send_sem=s, recv_sem=r, device_id=device, device_id_type=MESH)))

    def remote_sized(shapes, src, dst, device, pair_of_sems):
        s, r = pair_of_sems

        def make(size):
            return lambda: pltpu.make_async_remote_copy(src_ref=src(*size), dst_ref=dst(*size), send_sem=s, recv_sem=r, device_id=device, device_id_type=MESH)

        return Copy(*((cond, make(size)) for cond, size in shapes))

    def row_big(q):
        return (q < 2) == (c == 0)

    def row_at(q):
        return pl.multiple_of(56 * q + 8 * jnp.where(c == 0, jnp.minimum(q, 2), jnp.maximum(q - 2, 0)), 8)

    def col_big(q):
        return jnp.where(c == 0, q, 3 - q) < 3

    def col_at(q):
        return pl.multiple_of(384 * q + 128 * jnp.where(c == 0, jnp.minimum(q, 3), jnp.maximum(q - 1, 0)), 128)

    def rows_of(q):
        big = row_big(q)
        return [(big, (64,)), (jnp.logical_not(big), (56,))]

    def cols_of(q):
        big = col_big(q)
        return [(big, (512,)), (jnp.logical_not(big), (384,))]

    def cells_of(qx, qz):
        rb, cb = row_big(qx), col_big(qz)
        nr, nc = jnp.logical_not(rb), jnp.logical_not(cb)
        return [(rb & cb, (64, 512)), (rb & nc, (64, 384)), (nr & cb, (56, 512)), (nr & nc, (56, 384))]

    for part in range(2):
        for j in range(2):
            lraw[part, j, ROWS:PAD, :] = jnp.zeros((PAD - ROWS, V), F32)
    for part in range(4):
        for j in range(2):
            traw[part, j, ROWS:PAD, :] = jnp.zeros((PAD - ROWS, V), F32)

    @pl.when(jnp.logical_not(col_big(z)))
    def _():
        lz[:, :, :, :, 384:512] = jnp.zeros((4, 4, 2, 64, 128), F32)
        tx[:, :, :, :, 384:512] = jnp.zeros((4, 4, 2, 64, 128), F32)

    barrier = pltpu.get_barrier_semaphore()
    peers = [at_x(d) for d in (1, 2, 3)] + [at_z(d) for d in (1, 2, 3)] + [at_y(d) for d in (1, 2, 3)] + [other]
    for peer in peers:
        pl.semaphore_signal(barrier, inc=1, device_id=peer, device_id_type=MESH)
    pl.semaphore_wait(barrier, len(peers))

    def cut(i):
        j, k = divmod(i, KPARTS)
        return j, pl.ds(KC * k, KC)

    y_lambda, y_amps, forward = [], [], []
    for i in range(STEPS):
        j, cols = cut(i)
        y_lambda.append(remote(lambda j=j, cols=cols: l_ref.at[j, :, cols], lambda j=j, cols=cols: lraw.at[1, j, pl.ds(0, ROWS), cols], to_l, sems.take()))
        y_amps.append(remote(lambda j=j, cols=cols: t_ref.at[j, :, cols], lambda j=j, cols=cols: traw.at[2 + c, j, pl.ds(0, ROWS), cols], to_t, sems.take()))
        here = lambda j=j, cols=cols: traw.at[2 + c, j, pl.ds(0, ROWS), cols]
        forward.append(remote(here, here, other, sems.take()))
    core_amps = [remote(lambda j=j: t_ref.at[j], lambda j=j: traw.at[c, j, pl.ds(0, ROWS), :], other, sems.take()) for j in range(2)]
    own = []
    for j in range(2):
        own.append(pltpu.make_async_copy(l_ref.at[j], lraw.at[0, j, pl.ds(0, ROWS), :], local.at[2 * j]))
        own.append(pltpu.make_async_copy(t_ref.at[j], traw.at[c, j, pl.ds(0, ROWS), :], local.at[2 * j + 1]))

    hop_l = [
        remote_sized(
            rows_of(ring(x + d)),
            lambda r, d=d: l_ref.at[:, pl.ds(row_at(ring(x + d)), r), :],
            lambda r, d=d: lx.at[d - 1, :, pl.ds(0, r), :],
            at_x(d), sems.take(),
        )
        for d in (1, 2, 3)
    ]
    hop_t = [
        remote_sized(
            cols_of(ring(z + d)),
            lambda n, d=d: t_ref.at[:, :, pl.ds(col_at(ring(z + d)), n)],
            lambda n, d=d: tz.at[d - 1, :, :, pl.ds(0, n)],
            at_z(d), sems.take(),
        )
        for d in (1, 2, 3)
    ]
    got_l = [
        remote_sized(rows_of(x), lambda r, d=d: lx.at[d - 1, :, pl.ds(0, r), :], lambda r, d=d: lx.at[d - 1, :, pl.ds(0, r), :], at_x(d), (send.at[6 * 3 + 2 + d - 1], recv.at[6 * 3 + 2 + d - 1]))
        for d in (1, 2, 3)
    ]
    got_t = [
        remote_sized(cols_of(z), lambda n, d=d: tz.at[d - 1, :, :, pl.ds(0, n)], lambda n, d=d: tz.at[d - 1, :, :, pl.ds(0, n)], at_z(d), (send.at[6 * 3 + 5 + d - 1], recv.at[6 * 3 + 5 + d - 1]))
        for d in (1, 2, 3)
    ]

    second_l, second_t, got2_l, got2_t, keep_l, keep_t = {}, {}, {}, {}, {}, {}
    for d in range(4):

        def from_l(r, n, q, d=d):
            if d == 0:
                return l_ref.at[:, pl.ds(row_at(x), r), pl.ds(col_at(q), n)]
            return lx.at[d - 1, :, pl.ds(0, r), pl.ds(col_at(q), n)]

        def from_t(r, n, q, d=d):
            if d == 0:
                return t_ref.at[:, pl.ds(row_at(q), r), pl.ds(col_at(z), n)]
            return tz.at[d - 1, :, pl.ds(row_at(q), r), pl.ds(0, n)]

        for e in (1, 2, 3):
            s_l, s_t = sems.take(), sems.take()
            second_l[d, e] = remote_sized(
                cells_of(x, ring(z + e)),
                lambda r, n, d=d, e=e, f=from_l: f(r, n, ring(z + e)),
                lambda r, n, d=d: lz.at[ring(x - d), z, :, pl.ds(0, r), pl.ds(0, n)],
                at_z(e), s_l,
            )
            second_t[d, e] = remote_sized(
                cells_of(ring(x + e), z),
                lambda r, n, d=d, e=e, f=from_t: f(r, n, ring(x + e)),
                lambda r, n, d=d: tx.at[x, ring(z - d), :, pl.ds(0, r), pl.ds(0, n)],
                at_x(e), s_t,
            )
            land_l = lambda r, n, d=d, e=e: lz.at[ring(x - d), ring(z - e), :, pl.ds(0, r), pl.ds(0, n)]
            land_t = lambda r, n, d=d, e=e: tx.at[ring(x - e), ring(z - d), :, pl.ds(0, r), pl.ds(0, n)]
            got2_l[d, e] = remote_sized(cells_of(x, z), land_l, land_l, at_z(e), s_l)
            got2_t[d, e] = remote_sized(cells_of(x, z), land_t, land_t, at_x(e), s_t)

        def make_l(r, n, d=d, f=from_l):
            return lambda: pltpu.make_async_copy(f(r, n, z), lz.at[ring(x - d), z, :, pl.ds(0, r), pl.ds(0, n)], local.at[4 + d])

        def make_t(r, n, d=d, f=from_t):
            return lambda: pltpu.make_async_copy(f(r, n, x), tx.at[x, ring(z - d), :, pl.ds(0, r), pl.ds(0, n)], local.at[8 + d])

        keep_l[d] = Copy(*((cond, make_l(*size)) for cond, size in cells_of(x, z)))
        keep_t[d] = Copy(*((cond, make_t(*size)) for cond, size in cells_of(x, z)))

    for copy in own:
        copy.start()
    for i in range(STEPS):
        y_lambda[i].start()
        y_amps[i].start()
        if i == 0:
            for d in (0, 2, 1):
                hop_l[d].start()
                hop_t[d].start()
            core_amps[0].start()
            core_amps[1].start()
    for e in (1, 3, 2):
        second_l[0, e].start()
        second_t[0, e].start()
    keep_l[0].start()
    keep_t[0].start()

    acc[...] = jnp.zeros_like(acc)

    def multiply(i):
        j, cols = cut(i)
        for part in range(2):

            @pl.loop(0, PAD // 32)
            def _(b, part=part):
                at = pl.multiple_of(b * 32, 32)
                hi, lo = split(lraw[part, j, pl.ds(at, 32), cols])
                rows = pl.ds(part * PAD + at, 32)
                lcat[rows, 0:KC] = hi
                lcat[rows, KC : 2 * KC] = lo
                lcat[rows, 2 * KC :] = hi

        for slot in range(8):

            @pl.loop(0, 4)
            def _(b, slot=slot):
                at = pl.multiple_of(b * 32, 32)
                hi, lo = split(traw[slot // 2, j, pl.ds(120 * (slot % 2) + at, 32), cols])
                rows = pl.ds(slot * 128 + at, 32)
                tcat[rows, 0:KC] = hi
                tcat[rows, KC : 2 * KC] = hi
                tcat[rows, 2 * KC :] = lo

        @pl.loop(0, 4)
        def _(n):
            rhs = tcat[pl.ds(pl.multiple_of(n * 256, 256), 256), :]

            @pl.loop(0, 2)
            def _(m):
                rows = pl.ds(pl.multiple_of(m * 256, 256), 256)
                r = dot_nt(lcat[rows, :], rhs)
                acc[n // 2, 2 * (n % 2), rows, :] += r[:, :128]
                acc[n // 2, 2 * (n % 2) + 1, rows, :] += r[:, 128:]

    for copy in own:
        copy.wait()
    for i in range(STEPS):
        y_amps[i].wait_recv()
        forward[i].start()
        y_lambda[i].wait_recv()
        if i % KPARTS == 0:
            core_amps[i // KPARTS].wait_recv()
        forward[i].wait_recv()
        multiply(i)
        if i == 2:
            for d in (1, 3, 2):
                got_l[d - 1].wait_recv()
                for e in (1, 3, 2):
                    second_l[d, e].start()
                keep_l[d].start()
                got_t[d - 1].wait_recv()
                for e in (1, 3, 2):
                    second_t[d, e].start()
                keep_t[d].start()

    part_o, part_p, cells_o, cells_p, last, y_move = {}, {}, {}, {}, {}, None
    for d in (1, 2, 3):
        part_o[d] = remote(lambda d=d: acc.at[:, ring(z + d), pl.ds(0, 256), :], lambda d=d: ro1.at[d - 1], at_z(d), sems.take())
        part_p[d] = remote(lambda d=d: acc.at[:, :, pl.ds(pl.multiple_of(256 + 64 * ring(x + d), 64), 64), :], lambda d=d: rp1.at[d - 1], at_x(d), sems.take())
        cells_o[d] = remote(lambda d=d: so.at[:, pl.ds(pl.multiple_of(64 * ring(x + d), 64), 64), :], lambda d=d: ro2.at[d - 1], at_x(d), sems.take())
        cells_p[d] = remote(lambda d=d: sp.at[:, ring(z + d)], lambda d=d: rp2.at[d - 1], at_z(d), sems.take())
    y_move = remote(lambda: fp, lambda: yq, to_l, sems.take())
    for d in (1, 3, 2):
        part_o[d].start()
        part_p[d].start()

    for d in range(4):
        keep_l[d].wait()
        keep_t[d].wait()
        for e in (1, 2, 3):
            got2_l[d, e].wait_recv()
            got2_t[d, e].wait_recv()
    gram[...] = jnp.zeros_like(gram)

    @pl.loop(0, jnp.where(row_big(x), 8, 7))
    def _(b):
        rows = pl.ds(pl.multiple_of(b * 8, 8), 8)
        a_hi, a_lo = split(lz[:, :, :, rows, :].reshape(256, 512))
        b_hi, b_lo = split(tx[:, :, :, rows, :].reshape(256, 512))
        gram[...] += dot_nt(a_hi, b_hi) + (dot_nt(a_lo, b_hi) + dot_nt(a_hi, b_lo))

    row = lax.broadcasted_iota(jnp.int32, (256, 256), 0)
    col = lax.broadcasted_iota(jnp.int32, (256, 256), 1)
    same = lax.rem(row, 8) == lax.rem(col, 8)
    by_row = jnp.where(same, gram[...], 0.0).reshape(NP, 8, 256).sum(axis=1)
    pick = lax.broadcasted_iota(jnp.int32, (256, 128), 0)
    pick = (lax.div(pick, 8) == lax.broadcasted_iota(jnp.int32, (256, 128), 1)).astype(F32)
    inter = lax.dot_general(by_row, pick, (((1,), (0,)), ((), ())), precision=lax.Precision.HIGHEST, preferred_element_type=F32)

    def share(buf, me, places, value):
        buf[me] = value
        copies = []
        for d, place in places:
            copy = remote(lambda: buf.at[me], lambda: buf.at[me], place, sems.take())
            copy.start()
            copies.append(copy)
        return copies

    def total(buf, copies, n):
        for copy in copies:
            copy.wait_recv()
        value = buf[0]
        for k in range(1, n):
            value = value + buf[k]
        return value

    over_x = share(ix, x, [(d, at_x(d)) for d in (1, 2, 3)], inter)

    for d in (1, 3, 2):
        part_o[d].wait_recv()
    for part in range(2):
        so[part] = (acc[part, z, 0:256, :] + ro1[0, part]) + (ro1[1, part] + ro1[2, part])
    for d in (1, 3, 2):
        cells_o[d].start()
    for d in (1, 3, 2):
        part_p[d].wait_recv()
    mine = pl.ds(pl.multiple_of(256 + 64 * x, 64), 64)
    for part in range(2):
        for q in range(4):
            sp[part, q] = (acc[part, q, mine, :] + rp1[0, part, q]) + (rp1[1, part, q] + rp1[2, part, q])
    for d in (1, 3, 2):
        cells_p[d].start()

    over_z = share(iz, z, [(d, at_z(d)) for d in (1, 2, 3)], total(ix, over_x, 4))

    for d in (1, 3, 2):
        cells_p[d].wait_recv()
    for part in range(2):
        fp[part] = (sp[part, z] + rp2[0, part]) + (rp2[1, part] + rp2[2, part])
    y_move.start()
    for d in (1, 3, 2):
        cells_o[d].wait_recv()
    mine = pl.ds(pl.multiple_of(64 * x, 64), 64)
    for part in range(2):
        fo[part] = (so[part, mine, :] + ro2[0, part]) + (ro2[1, part] + ro2[2, part])

    lasts = []
    for src, b in ((fo, y), (fo, y_t), (yq, y_l), (yq, 3 - y_l)):
        k = len(lasts)
        s = sems.take()
        block = lambda src=src, k=k: src.at[k % 2]
        away, stays = b != x, b == x
        go = Copy((away, lambda block=block, b=b, s=s: pltpu.make_async_remote_copy(src_ref=block(), dst_ref=fin.at[x], send_sem=s[0], recv_sem=recv.at[N_SEMS - 4 + x], device_id=dev(b, z, y, c), device_id_type=MESH)))
        stay = Copy((stays, lambda block=block: pltpu.make_async_copy(block(), fin.at[x], local.at[12])))
        lasts.append((go, stay))
    for go, stay in lasts[:2]:
        go.start()
        stay.start()
    over_y = share(iy, y, [(d, at_y(d)) for d in (1, 2, 3)], total(iz, over_z, 4))
    y_move.wait_recv()
    for go, stay in lasts[2:]:
        go.start()
        stay.start()
    over_c = share(ic, c, [(1, other)], total(iy, over_y, 4))
    for go, stay in lasts:
        stay.wait()
    for d in (1, 2, 3):
        q = ring(x - d)
        pltpu.make_async_remote_copy(src_ref=fin.at[q], dst_ref=fin.at[q], send_sem=send.at[0], recv_sem=recv.at[N_SEMS - 4 + q], device_id=at_x(d), device_id_type=MESH).wait_recv()
    out_ref[...] = fin[...].reshape(256, 128)[:ROWS, :120]
    inter_ref[...] = total(ic, over_c, 2)

    sent = y_lambda + y_amps + forward + core_amps + hop_l + hop_t + list(second_l.values()) + list(second_t.values())
    sent += [y_move] + [go for go, _ in lasts] + over_x + over_z + over_y + over_c
    for group in (part_o, part_p, cells_o, cells_p):
        sent += list(group.values())
    for copy in sent:
        copy.wait_send()


def shards(lambda_blocks, amplitudes, pair_list):
    highest = lax.Precision.HIGHEST
    vmem = lambda shape, dtype=F32: pltpu.VMEM(shape, dtype)
    density_virt, intersection = pl.pallas_call(
        kernel,
        out_shape=(jax.ShapeDtypeStruct((ROWS, 120), F32), jax.ShapeDtypeStruct((NP, 128), F32)),
        in_specs=[pl.BlockSpec(memory_space=pl.ANY)] * 2,
        out_specs=(pl.BlockSpec(memory_space=pltpu.VMEM),) * 2,
        scratch_shapes=[
            vmem((2, 2, PAD, V)), vmem((4, 2, PAD, V)), vmem((512, 3 * KC), BF16), vmem((1024, 3 * KC), BF16), vmem((2, 4, 512, 128)),
            vmem((3, 2, 64, V)), vmem((3, 2, ROWS, 512)), vmem((4, 4, 2, 64, 512)), vmem((4, 4, 2, 64, 512)), vmem((256, 256)),
            vmem((3, 2, 256, 128)), vmem((3, 2, 64, 128)), vmem((3, 2, 4, 64, 128)), vmem((3, 2, 64, 128)),
            vmem((2, 256, 128)), vmem((2, 4, 64, 128)), vmem((2, 64, 128)), vmem((2, 64, 128)), vmem((2, 64, 128)), vmem((4, 64, 128)),
            vmem((4, NP, 128)), vmem((4, NP, 128)), vmem((4, NP, 128)), vmem((2, NP, 128)),
            pltpu.SemaphoreType.DMA((N_SEMS,)), pltpu.SemaphoreType.DMA((N_SEMS,)), pltpu.SemaphoreType.DMA((13,)),
        ],
        compiler_params=pltpu.CompilerParams(collective_id=0, has_side_effects=True, vmem_limit_bytes=60 * 2**20),
        cost_estimate=pl.CostEstimate(flops=12_000_000_000, bytes_accessed=8_000_000, transcendentals=0),
    )(lambda_blocks, amplitudes)
    intersection = intersection[:, :NP]
    first = pair_list[:, 0]
    second = pair_list[:, 1]
    one_hot = (first[:, None] == jnp.arange(OCC, dtype=jnp.int32)[None, :]).astype(F32)
    same_k = (second[:, None] == second[None, :]).astype(F32)
    inner = jnp.dot(same_k * intersection, one_hot, precision=highest)
    density_occ = -jnp.dot(one_hot.T, inner, precision=highest)
    return (density_virt, density_occ)


def solution(mesh):
    in_specs = (P("pair", "virt", None), P("pair", "virt", None), P())
    out_specs = (P("virt", "pair"), P())
    return jax.shard_map(shards, mesh=mesh, in_specs=in_specs, out_specs=out_specs, check_vma=False)
```

time: 284 us -> 129 us (0.45)
  Pallas kernels: 0 us -> 122 us
  waiting for transfers between devices: 110 us -> 0 us
  blocking collectives: 65.9 us -> 0 us
  matrix products: 40.8 us -> 1.97 us
  local copies, waits for them, and re-layouts: 30.9 us -> 2.31 us
  starting transfers between devices: 18.5 us -> 0 us
  between operations: 14.8 us -> 0.65 us
    pallas_call x0 -> x1, Pallas kernels: none -> 122 us  [shards(): pl.pallas_call(kernel, out_shape=(jax.ShapeDtypeStruct((ROWS, 120), F32),...]
    psum x1 -> x0, blocking collectives: 65.9 us -> none  [shards(): intersection = lax.psum(intersection_part, ('pair', 'virt'))]
    all_gather x1 -> x0, waiting for transfers between devices: 59.4 us -> none  [shards(): lax.all_gather(amplitudes, 'virt', axis=1, tiled=True)]
    all_to_all x2 -> x0, waiting for transfers between devices: 50 us -> none  [the longest x1 50 us: shards(): lax.all_to_all(amplitudes, 'pair', split_axis=2, concat_axis=0, tiled=True)]
    dot_general x2 -> x0, matrix products: 39.6 us -> none  [the longest x1 30.7 us: shards(): jnp.einsum('pac,pbc->ab', lambda_blocks, lax.all_gather(amplitudes, 'virt...]
    all_to_all x2 -> x0, starting transfers between devices: 18.4 us -> none  [the longest x1 10.5 us: shards(): lax.all_to_all(lambda_blocks, 'pair', split_axis=2, concat_axis=0, tiled=...]
    unnamed x8 -> x1, local copies, waits for them, and re-layouts: 16.8 us -> 1.56 us
    all_to_all x2 -> x0, local copies, waits for them, and re-layouts: 14.2 us -> none  [the longest x1 7.09 us: shards(): lax.all_to_all(lambda_blocks, 'pair', split_axis=2, concat_axis=0, tiled=...]
  transfers between devices with their start and end apart: 4 -> 0, of which waited for: 2 -> 0; matrix products, arithmetic and copies ran while one was open for 25% -> 0% of each run, Pallas kernels for 0% -> 0%
where the time goes in v1:
time: 129 us; the launch traced here: 127 us
  Pallas kernels  122 us (95%)
  local copies, waits for them, and re-layouts  2.31 us (2%)
  matrix products  1.97 us (2%)
    pallas_call x1, Pallas kernels, shards(): pl.pallas_call(kernel, out_shape=(jax.ShapeDtypeStruct((ROWS, 120), F32),...  122 us

profile of v1, /device:TPU:16, one launch (start us, length us, event | category | flops | bytes accessed | tf_op | source)
XLA Modules:
  0.0 127.3 jit_solution(8045100528827450109)
XLA Ops:
  0.6 0.8 slice_bitcast_fusion
  1.4 122.3 %shard_map.50 = (f32[240,120]{1,0:T(8,128)}, f32[32,128]{1,0:T(8,128)}) custom-call(f32[2,240,1920]{2,1,0:T(8,128)} %l_ref.1, f32[2,240,1920]{2,1,0:T(8,128)} %t_ref.1), custom_call_target="tpu_custom_call" | custom-call | flops 12000000000 | bytes 8000000 | tf_op jit(solution)/shard_map/pallas_call | solution.py:436
  123.7 0.9 fusion
  124.7 1.1 convolution_negate_fusion
  125.7 1.6 %copy.6 = f32[240,120]{1,0:T(8,128)} copy(f32[240,120]{1,0:T(8,128)} %get-tuple-element.10) | data formatting | bytes 230400

commit v2 on v1

v2 whole, which is shorter than its diff:
```python
import jax
import jax.numpy as jnp
from jax import lax
from jax.experimental import pallas as pl
from jax.experimental.pallas import tpu as pltpu
from jax.sharding import PartitionSpec as P

OCC = 200
NP = 32
ROWS = 240
PAD = 256
V = 1920
CUTS = ((0, 0, 640), (0, 640, 640), (0, 1280, 640), (1, 0, 640), (1, 640, 640), (1, 1280, 384), (1, 1664, 256))
OWN_CUTS = ((0, 0, 640), (0, 640, 640), (0, 1280, 640), (1, 0, 640), (1, 640, 640), (1, 1280, 640))
KC = 640
STEPS = len(CUTS)
MESH = pl.DeviceIdType.MESH
F32 = jnp.float32
BF16 = jnp.bfloat16


class Copy:
    def __init__(self, *variants):
        self.variants = variants

    def _each(self, act):
        for cond, make in self.variants:
            if cond is None:
                act(make())
            else:

                @pl.when(cond)
                def _(make=make):
                    act(make())

    def start(self):
        self._each(lambda c: c.start())

    def wait_send(self):
        self._each(lambda c: c.wait_send())

    def wait_recv(self):
        self._each(lambda c: c.wait_recv())

    def wait(self):
        self._each(lambda c: c.wait())


class Sems:
    def __init__(self, send, recv):
        self.send, self.recv, self.n = send, recv, 0

    def take(self):
        self.n += 1
        return self.send.at[self.n - 1], self.recv.at[self.n - 1]


def split(v):
    hi = v.astype(BF16)
    return hi, (v - hi.astype(F32)).astype(BF16)


NT = (((1,), (1,)), ((), ()))


def dot_nt(a, b):
    return lax.dot_general(a, b, NT, preferred_element_type=F32)


N_SEMS = 160


def kernel(
    l_ref, t_ref, pair_ref, fin, occ_ref,
    lraw, traw, lcat, tcat, acc, lx, tz, lz, tx, gram,
    rz1, rx1, rz2, rx2, sz, sx, done, ig, ip, pair_list,
    send, recv, local,
):
    pair, virt = lax.axis_index("pair"), lax.axis_index("virt")
    x, z = lax.div(pair, 4), lax.rem(pair, 4)
    y, c = lax.div(virt, 2), lax.rem(virt, 2)
    sems = Sems(send, recv)

    def ring(a):
        return lax.rem(a + 4, 4)

    def dev(xx, zz, yy, cc):
        return (xx * 4 + zz, yy * 2 + cc)

    def at_x(d):
        return dev(ring(x + d), z, y, c)

    def at_z(d):
        return dev(x, ring(z + d), y, c)

    def at_y(d):
        return dev(x, z, ring(y + d), c)

    other = dev(x, z, y, 1 - c)
    y_l = y + 1 - 2 * lax.rem(y, 2)
    y_t = 3 - y
    to_l, to_t = dev(x, z, y_l, c), dev(x, z, y_t, c)

    def remote(src, dst, device, pair_of_sems):
        s, r = pair_of_sems
        return Copy((None, lambda: pltpu.make_async_remote_copy(src_ref=src(), dst_ref=dst(), send_sem=s, recv_sem=r, device_id=device, device_id_type=MESH)))

    def remote_sized(shapes, src, dst, device, pair_of_sems):
        s, r = pair_of_sems

        def make(size):
            return lambda: pltpu.make_async_remote_copy(src_ref=src(*size), dst_ref=dst(*size), send_sem=s, recv_sem=r, device_id=device, device_id_type=MESH)

        return Copy(*((cond, make(size)) for cond, size in shapes))

    def row_big(q):
        return (q < 2) == (c == 0)

    def row_at(q):
        return pl.multiple_of(56 * q + 8 * jnp.where(c == 0, jnp.minimum(q, 2), jnp.maximum(q - 2, 0)), 8)

    def col_big(q):
        return lax.div(q, 2) != c

    def col_at(q):
        return pl.multiple_of(512 * q - 128 * jnp.where((c == 0) & (q > 1), 1, 0), 128)

    shared = pl.ds(pl.multiple_of(384 + 1024 * c, 128), 128)
    aside = pl.ds(384, 128)

    def shared_at(q):
        return 32 * (1 - lax.rem(q, 2))

    def shared_of(qx, qz):
        short, odd, big = jnp.logical_not(col_big(qz)), lax.rem(qz, 2) == 1, row_big(qx)
        narrow = jnp.logical_not(odd) & jnp.logical_not(big)
        return [(short & jnp.logical_not(narrow), (32,)), (short & narrow, (24,))]

    def some(at, r):
        return pl.ds(pl.multiple_of(at, 8), r)

    def rows_of(q):
        big = row_big(q)
        return [(big, (64,)), (jnp.logical_not(big), (56,))]

    def cols_of(q):
        big = col_big(q)
        return [(big, (512,)), (jnp.logical_not(big), (384,))]

    def cells_of(qx, qz):
        rb, cb = row_big(qx), col_big(qz)
        nr, nc = jnp.logical_not(rb), jnp.logical_not(cb)
        return [(rb & cb, (64, 512)), (rb & nc, (64, 384)), (nr & cb, (56, 512)), (nr & nc, (56, 384))]

    barrier = pltpu.get_barrier_semaphore()
    around = [(dy, dc) for dy in range(4) for dc in range(2) if (dy, dc) != (0, 0)]
    plane = [(dx, dz) for dx in range(4) for dz in range(4) if (dx, dz) != (0, 0)]
    at_group = [dev(x, z, ring(y + dy), lax.rem(c + dc, 2)) for dy, dc in around]
    at_plane = [dev(ring(x + dx), ring(z + dz), y, c) for dx, dz in plane]
    peers = at_group + at_plane + [dev(ring(x + d), z, y_l, c) for d in (1, 2, 3)]
    for peer in peers:
        pl.semaphore_signal(barrier, inc=1, device_id=peer, device_id_type=MESH)
    pl.semaphore_wait(barrier, len(peers))

    def cut(i):
        j, first, n = CUTS[i]
        return j, pl.ds(first, n)

    y_lambda, y_amps, forward = [], [], []
    for i in range(STEPS):
        j, cols = cut(i)
        y_lambda.append(remote(lambda j=j, cols=cols: l_ref.at[j, :, cols], lambda j=j, cols=cols: lraw.at[1, j, pl.ds(0, ROWS), cols], to_l, sems.take()))
        y_amps.append(remote(lambda j=j, cols=cols: t_ref.at[j, :, cols], lambda j=j, cols=cols: traw.at[2 + c, j, pl.ds(0, ROWS), cols], to_t, sems.take()))
        here = lambda j=j, cols=cols: traw.at[2 + c, j, pl.ds(0, ROWS), cols]
        forward.append(remote(here, here, other, sems.take()))
    core_amps = [remote(lambda j=j: t_ref.at[j], lambda j=j: traw.at[c, j, pl.ds(0, ROWS), :], other, sems.take()) for j in range(2)]
    own = []
    for j in range(2):
        own.append(pltpu.make_async_copy(l_ref.at[j], lraw.at[0, j, pl.ds(0, ROWS), :], local.at[2 * j]))
        own.append(pltpu.make_async_copy(t_ref.at[j], traw.at[c, j, pl.ds(0, ROWS), :], local.at[2 * j + 1]))

    hop_l = [
        remote_sized(
            rows_of(ring(x + d)),
            lambda r, d=d: l_ref.at[:, pl.ds(row_at(ring(x + d)), r), :],
            lambda r, d=d: lx.at[d - 1, :, pl.ds(0, r), :],
            at_x(d), sems.take(),
        )
        for d in (1, 2, 3)
    ]
    hop_t = [
        remote_sized(
            cols_of(ring(z + d)),
            lambda n, d=d: t_ref.at[:, :, pl.ds(col_at(ring(z + d)), n)],
            lambda n, d=d: tz.at[d - 1, :, :, pl.ds(0, n)],
            at_z(d), sems.take(),
        )
        for d in (1, 2, 3)
    ]
    hop_s, got_s = {}, {}
    for d in (1, 2, 3):
        for q in range(4):
            s_q = sems.take()
            to = ring(z + d)
            hop_s[d, q] = remote_sized(
                shared_of(q, to),
                lambda r, q=q, to=to: t_ref.at[:, some(row_at(q) + shared_at(to), r), shared],
                lambda r, d=d, q=q, to=to: tz.at[d - 1, :, some(row_at(q) + shared_at(to), r), aside],
                at_z(d), s_q,
            )
            land = lambda r, d=d, q=q: tz.at[d - 1, :, some(row_at(q) + shared_at(z), r), aside]
            got_s[d, q] = remote_sized(shared_of(q, z), land, land, at_z(d), s_q)
    got_l = [
        remote_sized(rows_of(x), lambda r, d=d: lx.at[d - 1, :, pl.ds(0, r), :], lambda r, d=d: lx.at[d - 1, :, pl.ds(0, r), :], at_x(d), (send.at[3 * STEPS + 2 + d - 1], recv.at[3 * STEPS + 2 + d - 1]))
        for d in (1, 2, 3)
    ]
    got_t = [
        remote_sized(cols_of(z), lambda n, d=d: tz.at[d - 1, :, :, pl.ds(0, n)], lambda n, d=d: tz.at[d - 1, :, :, pl.ds(0, n)], at_z(d), (send.at[3 * STEPS + 5 + d - 1], recv.at[3 * STEPS + 5 + d - 1]))
        for d in (1, 2, 3)
    ]

    more_l, more_t, got_more_l, got_more_t, hold = {}, {}, {}, {}, {}
    second_l, second_t, got2_l, got2_t, keep_l, keep_t = {}, {}, {}, {}, {}, {}
    for d in range(4):

        def from_l(r, n, q, d=d):
            if d == 0:
                return l_ref.at[:, pl.ds(row_at(x), r), pl.ds(col_at(q), n)]
            return lx.at[d - 1, :, pl.ds(0, r), pl.ds(col_at(q), n)]

        def from_t(r, n, q, d=d):
            if d == 0:
                return t_ref.at[:, pl.ds(row_at(q), r), pl.ds(col_at(z), n)]
            return tz.at[d - 1, :, pl.ds(row_at(q), r), pl.ds(0, n)]

        def shared_l(r, q, d=d):
            if d == 0:
                return l_ref.at[:, some(row_at(x) + shared_at(q), r), shared]
            return lx.at[d - 1, :, some(shared_at(q), r), shared]

        def shared_t(r, q, d=d):
            if d == 0:
                return t_ref.at[:, some(row_at(q) + shared_at(z), r), shared]
            return tz.at[d - 1, :, some(row_at(q) + shared_at(z), r), aside]

        for e in (1, 2, 3):
            s_l, s_t = sems.take(), sems.take()
            qx, qz = ring(x + e), ring(z + e)
            more_l[d, e] = remote_sized(
                shared_of(x, qz),
                lambda r, qz=qz, f=shared_l: f(r, qz),
                lambda r, d=d, qz=qz: lz.at[ring(x - d), z, :, some(shared_at(qz), r), aside],
                at_z(e), s_l,
            )
            more_t[d, e] = remote_sized(
                shared_of(qx, z),
                lambda r, qx=qx, f=shared_t: f(r, qx),
                lambda r, d=d: tx.at[x, ring(z - d), :, some(shared_at(z), r), aside],
                at_x(e), s_t,
            )
            land_l = lambda r, d=d, e=e: lz.at[ring(x - d), ring(z - e), :, some(shared_at(z), r), aside]
            land_t = lambda r, d=d, e=e: tx.at[ring(x - e), ring(z - d), :, some(shared_at(z), r), aside]
            got_more_l[d, e] = remote_sized(shared_of(x, z), land_l, land_l, at_z(e), s_l)
            got_more_t[d, e] = remote_sized(shared_of(x, z), land_t, land_t, at_x(e), s_t)

        def hold_l(r, d=d, f=shared_l):
            return lambda: pltpu.make_async_copy(f(r, z), lz.at[ring(x - d), z, :, some(shared_at(z), r), aside], local.at[14 + d])

        def hold_t(r, d=d, f=shared_t):
            return lambda: pltpu.make_async_copy(f(r, x), tx.at[x, ring(z - d), :, some(shared_at(z), r), aside], local.at[18 + d])

        hold[d] = [Copy(*((cond, h(*size)) for cond, size in shared_of(x, z))) for h in (hold_l, hold_t)]

        for e in (1, 2, 3):
            s_l, s_t = sems.take(), sems.take()
            second_l[d, e] = remote_sized(
                cells_of(x, ring(z + e)),
                lambda r, n, d=d, e=e, f=from_l: f(r, n, ring(z + e)),
                lambda r, n, d=d: lz.at[ring(x - d), z, :, pl.ds(0, r), pl.ds(0, n)],
                at_z(e), s_l,
            )
            second_t[d, e] = remote_sized(
                cells_of(ring(x + e), z),
                lambda r, n, d=d, e=e, f=from_t: f(r, n, ring(x + e)),
                lambda r, n, d=d: tx.at[x, ring(z - d), :, pl.ds(0, r), pl.ds(0, n)],
                at_x(e), s_t,
            )
            land_l = lambda r, n, d=d, e=e: lz.at[ring(x - d), ring(z - e), :, pl.ds(0, r), pl.ds(0, n)]
            land_t = lambda r, n, d=d, e=e: tx.at[ring(x - e), ring(z - d), :, pl.ds(0, r), pl.ds(0, n)]
            got2_l[d, e] = remote_sized(cells_of(x, z), land_l, land_l, at_z(e), s_l)
            got2_t[d, e] = remote_sized(cells_of(x, z), land_t, land_t, at_x(e), s_t)

        def make_l(r, n, d=d, f=from_l):
            return lambda: pltpu.make_async_copy(f(r, n, z), lz.at[ring(x - d), z, :, pl.ds(0, r), pl.ds(0, n)], local.at[4 + d])

        def make_t(r, n, d=d, f=from_t):
            return lambda: pltpu.make_async_copy(f(r, n, x), tx.at[x, ring(z - d), :, pl.ds(0, r), pl.ds(0, n)], local.at[8 + d])

        keep_l[d] = Copy(*((cond, make_l(*size)) for cond, size in cells_of(x, z)))
        keep_t[d] = Copy(*((cond, make_t(*size)) for cond, size in cells_of(x, z)))

    pairs = pltpu.make_async_copy(pair_ref, pair_list, local.at[13])
    pairs.start()
    for copy in own:
        copy.start()
    for i in range(STEPS):
        y_lambda[i].start()
        y_amps[i].start()
        if i == 0:
            for d in (0, 2, 1):
                hop_l[d].start()
                hop_t[d].start()
                for q in range(4):
                    hop_s[d + 1, q].start()
            core_amps[0].start()
            core_amps[1].start()
    for e in (1, 3, 2):
        second_l[0, e].start()
        more_l[0, e].start()
        second_t[0, e].start()
        more_t[0, e].start()
    for copy in (keep_l[0], keep_t[0], *hold[0]):
        copy.start()

    for part in range(2):
        for j in range(2):
            lraw[part, j, ROWS:PAD, :] = jnp.zeros((PAD - ROWS, V), F32)
    for part in range(4):
        for j in range(2):
            traw[part, j, ROWS:PAD, :] = jnp.zeros((PAD - ROWS, V), F32)

    @pl.when(jnp.logical_not(col_big(z)))
    def _():
        empty = pl.ds(pl.multiple_of(32 - shared_at(z), 32), 32)
        lz[:, :, :, empty, aside] = jnp.zeros((4, 4, 2, 32, 128), F32)
        tx[:, :, :, empty, aside] = jnp.zeros((4, 4, 2, 32, 128), F32)

    acc[...] = jnp.zeros_like(acc)
    gram[...] = jnp.zeros_like(gram)

    def halves(j, first, n, blocks, parts_l, parts_t):
        cols = pl.ds(first, n)
        for part in parts_l:

            @pl.loop(0, PAD // 32)
            def _(b, part=part):
                at = pl.multiple_of(b * 32, 32)
                hi, lo = split(lraw[part, j, pl.ds(at, 32), cols])
                rows = pl.ds(part * PAD + at, 32)
                lcat[rows, 0:n] = hi
                lcat[rows, n : 2 * n] = lo
                lcat[rows, 2 * n : 3 * n] = hi

        for slot in parts_t:

            @pl.loop(0, 4)
            def _(b, slot=slot):
                at = pl.multiple_of(b * 32, 32)
                hi, lo = split(traw[slot // 2, j, pl.ds(120 * (slot % 2) + at, 32), cols])
                rows = pl.ds(slot * 128 + at, 32)
                tcat[rows, 0:n] = hi
                tcat[rows, n : 2 * n] = hi
                tcat[rows, 2 * n : 3 * n] = lo

        for n_range, m in blocks:

            @pl.loop(*n_range)
            def _(b, m=m):
                r = dot_nt(lcat[m * 256 : (m + 1) * 256, 0 : 3 * n], tcat[pl.ds(pl.multiple_of(b * 256, 256), 256), 0 : 3 * n])
                rows = slice(m * 256, (m + 1) * 256)
                acc[b // 2, 2 * (b % 2), rows, :] += r[:, :128]
                acc[b // 2, 2 * (b % 2) + 1, rows, :] += r[:, 128:]

    def lo(h):
        return pl.ds(256 * h, 128)

    def hi_of(h, q):
        return pl.ds(pl.multiple_of(256 * h + 128 + 32 * q, 32), 32)

    early, late, second = [], ([], []), ({}, {})
    for d in (1, 3, 2):
        qx, qz = ring(x + d), ring(z + d)
        early.append(remote(lambda qz=qz: acc.at[0, qz, lo(0), :], lambda d=d: rz1.at[d - 1, 0, 0], at_z(d), sems.take()))
        early.append(remote(lambda qx=qx: acc.at[0, :, hi_of(0, qx), :], lambda d=d: rx1.at[d - 1, 0, 0], at_x(d), sems.take()))
        late[0].append(remote(lambda qz=qz: acc.at[1, qz, lo(0), :], lambda d=d: rz1.at[d - 1, 0, 1], at_z(d), sems.take()))
        late[0].append(remote(lambda qx=qx: acc.at[1, :, hi_of(0, qx), :], lambda d=d: rx1.at[d - 1, 0, 1], at_x(d), sems.take()))
        late[1].append(remote(lambda qz=qz: acc.at[:, qz, lo(1), :], lambda d=d: rz1.at[d - 1, 1], at_z(d), sems.take()))
        late[1].append(remote(lambda qx=qx: acc.at[:, :, hi_of(1, qx), :], lambda d=d: rx1.at[d - 1, 1], at_x(d), sems.take()))
        for h in range(2):
            second[h]["z", d] = remote(lambda qx=qx, h=h: sz.at[h, :, pl.ds(pl.multiple_of(32 * qx, 32), 32), :], lambda d=d, h=h: rz2.at[d - 1, h], at_x(d), sems.take())
            second[h]["x", d] = remote(lambda qz=qz, h=h: sx.at[h, :, qz], lambda d=d, h=h: rx2.at[d - 1, h], at_z(d), sems.take())

    for copy in own:
        copy.wait()
    for k, (j, first, n) in enumerate(OWN_CUTS):
        if k % 3 == 0:
            core_amps[j].wait_recv()
        halves(j, first, n, [((0, 2), 0)], (0,), range(4))
    for copy in early:
        copy.start()
    for i in range(STEPS):
        y_amps[i].wait_recv()
        forward[i].start()
        y_lambda[i].wait_recv()
        forward[i].wait_recv()
        halves(*CUTS[i], [((0, 4), 1), ((2, 4), 0)], (0, 1), range(8))
        if i == 2:
            for d in (1, 3, 2):
                got_l[d - 1].wait_recv()
                for e in (1, 3, 2):
                    second_l[d, e].start()
                    more_l[d, e].start()
                keep_l[d].start()
                got_t[d - 1].wait_recv()
                for q in range(4):
                    got_s[d, q].wait_recv()
                for e in (1, 3, 2):
                    second_t[d, e].start()
                    more_t[d, e].start()
                keep_t[d].start()
                for copy in hold[d]:
                    copy.start()
    for copy in late[0] + late[1]:
        copy.start()

    for d in range(4):
        keep_l[d].wait()
        keep_t[d].wait()
        for copy in hold[d]:
            copy.wait()
        for e in (1, 2, 3):
            for came in (got2_l, got2_t, got_more_l, got_more_t):
                came[d, e].wait_recv()
    @pl.loop(0, jnp.where(row_big(x), 8, 7))
    def _(b):
        rows = pl.ds(pl.multiple_of(b * 8, 8), 8)
        a_hi, a_lo = split(lz[:, :, :, rows, :].reshape(256, 512))
        b_hi, b_lo = split(tx[:, :, :, rows, :].reshape(256, 512))
        gram[...] += dot_nt(a_hi, b_hi) + (dot_nt(a_lo, b_hi) + dot_nt(a_hi, b_lo))

    row = lax.broadcasted_iota(jnp.int32, (256, 256), 0)
    col = lax.broadcasted_iota(jnp.int32, (256, 256), 1)
    same = lax.rem(row, 8) == lax.rem(col, 8)
    by_row = jnp.where(same, gram[...], 0.0).reshape(NP, 8, 256).sum(axis=1)
    pick = lax.broadcasted_iota(jnp.int32, (256, 128), 0)
    lane = lax.broadcasted_iota(jnp.int32, (256, 128), 1)
    inter = jnp.zeros((8, 128), F32)
    for k in range(4):
        wanted = (lax.div(pick, 8) + 32 * k == lane).astype(F32)
        inter += lax.dot_general(by_row[8 * k : 8 * k + 8], wanted, (((1,), (0,)), ((), ())), precision=lax.Precision.HIGHEST, preferred_element_type=F32)

    def share(buf, me, places, value):
        buf[me] = value
        copies = [remote(lambda: buf.at[me], lambda: buf.at[me], place, sems.take()) for place in places]
        for copy in copies:
            copy.start()
        return copies

    def total(buf, copies, n):
        for copy in copies:
            copy.wait_recv()
        value = buf[0]
        for k in range(1, n):
            value = value + buf[k]
        return value

    over_group = share(ig, virt, at_group, inter)

    def sum_first(h):
        for copy in (early if h == 0 else []) + late[h]:
            copy.wait_recv()
        for b in range(2):
            sz[h, b] = (acc[b, z, lo(h), :] + rz1[0, h, b]) + (rz1[1, h, b] + rz1[2, h, b])
        for d in (1, 3, 2):
            second[h]["z", d].start()
        for b in range(2):
            for q in range(4):
                sx[h, b, q] = (acc[b, q, hi_of(h, x), :] + rx1[0, h, b, q]) + (rx1[1, h, b, q] + rx1[2, h, b, q])
        for d in (1, 3, 2):
            second[h]["x", d].start()

    lasts = []

    def sum_second(h):
        for copy in second[h].values():
            copy.wait_recv()
        mine = pl.ds(pl.multiple_of(32 * x, 32), 32)
        for b, q in ((0, y), (1, y_t)):
            done[h, b, 0] = (sz[h, b, mine, :] + rz2[0, h, b]) + (rz2[1, h, b] + rz2[2, h, b])
            done[h, b, 1] = (sx[h, b, z] + rx2[0, h, b]) + (rx2[1, h, b] + rx2[2, h, b])
            s = sems.take()[0]
            make = lambda b=b, q=q, s=s: pltpu.make_async_remote_copy(src_ref=done.at[h, b], dst_ref=fin.at[:, x], send_sem=s, recv_sem=recv.at[N_SEMS - 4 + x], device_id=dev(q, z, (y, y_l)[h], c), device_id_type=MESH)
            if h == 0:
                go = Copy((q != x, make))
                stay = Copy((q == x, lambda b=b: pltpu.make_async_copy(done.at[0, b], fin.at[:, x], local.at[12])))
                stay.start()
            else:
                go, stay = Copy((None, make)), Copy()
            go.start()
            lasts.append((go, stay))

    sum_first(0)
    over_plane = share(ip, pair, at_plane, total(ig, over_group, 8))
    sum_first(1)
    sum_second(0)
    sum_second(1)

    every = total(ip, over_plane, 16)
    matrix = jnp.concatenate([every[:, 32 * k : 32 * k + 32] for k in range(4)], axis=0)
    pairs.wait()
    first, kind = pair_list[0:1, :], pair_list[1:2, :]
    one_hot = (first == lax.broadcasted_iota(jnp.int32, (256, NP), 0)).astype(F32)
    kind = (kind == lax.broadcasted_iota(jnp.int32, (NP, NP), 0)).astype(F32)
    same_k = lax.dot_general(kind, kind, (((0,), (0,)), ((), ())), preferred_element_type=F32)
    highest = lax.Precision.HIGHEST
    outer = lax.dot_general(one_hot, same_k * matrix, (((1,), (0,)), ((), ())), precision=highest, preferred_element_type=F32)
    occ_ref[...] = -lax.dot_general(outer, one_hot, NT, precision=highest, preferred_element_type=F32)

    for go, stay in lasts:
        stay.wait()
    in_plane = (x == y) | (x == y_t)
    for q in range(4):
        came = Copy((jnp.logical_not(in_plane & (x == q)), lambda q=q: pltpu.make_async_remote_copy(src_ref=done.at[0, 0], dst_ref=fin.at[:, q], send_sem=send.at[0], recv_sem=recv.at[N_SEMS - 4 + q], device_id=to_l, device_id_type=MESH)))
        came.wait_recv()

    sent = y_lambda + y_amps + forward + core_amps + hop_l + hop_t + list(second_l.values()) + list(second_t.values())
    for group in (hop_s, more_l, more_t):
        sent += list(group.values())
    sent += early + late[0] + late[1] + list(second[0].values()) + list(second[1].values()) + [go for go, _ in lasts] + over_group + over_plane
    for copy in sent:
        copy.wait_send()


def finish(fin_ref, occ_in, virt_ref, occ_ref):
    virt_ref[...] = fin_ref[...].reshape(256, 128)[:ROWS, :120]
    occ_ref[...] = occ_in[:OCC, :OCC]


def shards(lambda_blocks, amplitudes, pair_list):
    vmem = lambda shape, dtype=F32: pltpu.VMEM(shape, dtype)
    fin, occ = pl.pallas_call(
        kernel,
        out_shape=(jax.ShapeDtypeStruct((2, 4, 32, 128), F32), jax.ShapeDtypeStruct((256, 256), F32)),
        in_specs=[pl.BlockSpec(memory_space=pl.ANY)] * 3,
        out_specs=(pl.BlockSpec(memory_space=pltpu.VMEM),) * 2,
        scratch_shapes=[
            vmem((2, 2, PAD, V)), vmem((4, 2, PAD, V)), vmem((512, 3 * KC), BF16), vmem((1024, 3 * KC), BF16), vmem((2, 4, 512, 128)),
            vmem((3, 2, 64, V)), vmem((3, 2, ROWS, 512)), vmem((4, 4, 2, 64, 512)), vmem((4, 4, 2, 64, 512)), vmem((256, 256)),
            vmem((3, 2, 2, 128, 128)), vmem((3, 2, 2, 4, 32, 128)), vmem((3, 2, 2, 32, 128)), vmem((3, 2, 2, 32, 128)),
            vmem((2, 2, 128, 128)), vmem((2, 2, 4, 32, 128)), vmem((2, 2, 2, 32, 128)), vmem((8, 8, 128)), vmem((16, 8, 128)), vmem((2, NP), jnp.int32),
            pltpu.SemaphoreType.DMA((N_SEMS,)), pltpu.SemaphoreType.DMA((N_SEMS,)), pltpu.SemaphoreType.DMA((22,)),
        ],
        compiler_params=pltpu.CompilerParams(collective_id=0, has_side_effects=True, vmem_limit_bytes=60 * 2**20),
        cost_estimate=pl.CostEstimate(flops=12_000_000_000, bytes_accessed=8_000_000, transcendentals=0),
    )(lambda_blocks, amplitudes, pair_list.T)
    return pl.pallas_call(
        finish,
        out_shape=(jax.ShapeDtypeStruct((ROWS, 120), F32), jax.ShapeDtypeStruct((OCC, OCC), F32)),
        in_specs=[pl.BlockSpec(memory_space=pltpu.VMEM)] * 2,
        out_specs=(pl.BlockSpec(memory_space=pltpu.VMEM),) * 2,
    )(fin, occ)


def solution(mesh):
    in_specs = (P("pair", "virt", None), P("pair", "virt", None), P())
    out_specs = (P("virt", "pair"), P())
    return jax.shard_map(shards, mesh=mesh, in_specs=in_specs, out_specs=out_specs, check_vma=False)
```

time: 129 us -> 119 us (0.922)
  Pallas kernels: 122 us -> 117 us
  local copies, waits for them, and re-layouts: 2.31 us -> 0 us
  matrix products: 1.97 us -> 0 us
    pallas_call x1 -> x2, Pallas kernels: 122 us -> 117 us  [the longest x1 115 us: shards(): pl.pallas_call(kernel, out_shape=(jax.ShapeDtypeStruct((2, 4, 32, 128), F...]
    dot_general x2 -> x0, matrix products: 1.97 us -> none  [the longest x1 1.05 us: shards(): density_occ = -jnp.dot(one_hot.T, inner, precision=highest)]
    unnamed x1 -> x0, local copies, waits for them, and re-layouts: 1.56 us -> none
where the time goes in v2:
time: 119 us; the launch traced here: 118 us
  Pallas kernels  117 us (98%)
    pallas_call x1, Pallas kernels, shards(): pl.pallas_call(kernel, out_shape=(jax.ShapeDtypeStruct((2, 4, 32, 128), F...  115 us

profile of v2, /device:TPU:16, one launch (start us, length us, event | category | flops | bytes accessed | tf_op | source)
XLA Modules:
  0.0 117.7 jit_solution(11167137497926029971)
XLA Ops:
  0.6 115.3 %shard_map.50 = (f32[2,4,32,128]{3,2,1,0:T(8,128)}, f32[256,256]{1,0:T(8,128)}) custom-call(f32[2,240,1920]{2,1,0:T(8,128)} %l_ref.1, f32[2,240,1920]{2,1,0:T(8,128)} %t_ref.1, s32[2,32]{1,0:T(2,128)} %bitcast.1), custom_call_target="tpu_custom_call" | custom-call | flops 12000000000 | bytes 8000000 | tf_op jit(solution)/shard_map/pallas_call | solution.py:541
  115.9 1.8 %shard_map.51 = (f32[240,120]{1,0:T(8,128)}, f32[200,200]{1,0:T(8,128)}) custom-call(f32[2,4,32,128]{3,2,1,0:T(8,128)} %get-tuple-element.4.fin_ref, f32[256,256]{1,0:T(8,128)} %get-tuple-element.5.occ_in), custom_call_target="tpu_custom_call" | custom-call | tf_op jit(solution)/shard_map/pallas_call | solution.py:556

commit v3 on v2

--- a/solution.py
+++ b/solution.py
@@ -10,8 +10,9 @@
 ROWS = 240
 PAD = 256
 V = 1920
-CUTS = ((0, 0, 640), (0, 640, 640), (0, 1280, 640), (1, 0, 640), (1, 640, 640), (1, 1280, 384), (1, 1664, 256))
-OWN_CUTS = ((0, 0, 640), (0, 640, 640), (0, 1280, 640), (1, 0, 640), (1, 640, 640), (1, 1280, 640))
+WIDE = ((0, 0, 640), (0, 640, 640), (0, 1280, 640), (1, 0, 640), (1, 640, 640), (1, 1280, 640))
+NARROW = WIDE[:5] + ((1, 1280, 384), (1, 1664, 256))
+CUTS = tuple((0, cut) for cut in WIDE) + tuple((1, cut) for cut in NARROW)
 KC = 640
 STEPS = len(CUTS)
 MESH = pl.DeviceIdType.MESH
@@ -67,11 +68,11 @@
     return lax.dot_general(a, b, NT, preferred_element_type=F32)
 
 
-N_SEMS = 160
+N_SEMS = 192
 
 
 def kernel(
-    l_ref, t_ref, pair_ref, fin, occ_ref,
+    l_ref, t_ref, t_halves, pair_ref, fin, occ_ref,
     lraw, traw, lcat, tcat, acc, lx, tz, lz, tx, gram,
     rz1, rx1, rz2, rx2, sz, sx, done, ig, ip, pair_list,
     send, recv, local,
@@ -162,22 +163,19 @@
         pl.semaphore_signal(barrier, inc=1, device_id=peer, device_id_type=MESH)
     pl.semaphore_wait(barrier, len(peers))
 
-    def cut(i):
-        j, first, n = CUTS[i]
-        return j, pl.ds(first, n)
-
     y_lambda, y_amps, forward = [], [], []
-    for i in range(STEPS):
-        j, cols = cut(i)
-        y_lambda.append(remote(lambda j=j, cols=cols: l_ref.at[j, :, cols], lambda j=j, cols=cols: lraw.at[1, j, pl.ds(0, ROWS), cols], to_l, sems.take()))
-        y_amps.append(remote(lambda j=j, cols=cols: t_ref.at[j, :, cols], lambda j=j, cols=cols: traw.at[2 + c, j, pl.ds(0, ROWS), cols], to_t, sems.take()))
-        here = lambda j=j, cols=cols: traw.at[2 + c, j, pl.ds(0, ROWS), cols]
+    for half, (j, first, n) in CUTS:
+        cols = pl.ds(first, n)
+        rows_l, rows_t = pl.ds(128 * half, (128, 112)[half]), pl.ds(64 * half, (64, 56)[half])
+        y_lambda.append(remote(lambda j=j, r=rows_l, k=cols: l_ref.at[j, r, k], lambda j=j, r=rows_l, k=cols: lraw.at[1, j, r, k], to_l, sems.take()))
+        here = lambda j=j, r=rows_t, k=cols: traw.at[2 + c, j, :, r, k]
+        y_amps.append(remote(lambda j=j, r=rows_t, k=cols: t_halves.at[j, :, r, k], here, to_t, sems.take()))
         forward.append(remote(here, here, other, sems.take()))
-    core_amps = [remote(lambda j=j: t_ref.at[j], lambda j=j: traw.at[c, j, pl.ds(0, ROWS), :], other, sems.take()) for j in range(2)]
+    core_amps = [remote(lambda j=j: t_halves.at[j], lambda j=j: traw.at[c, j, :, pl.ds(0, 120), :], other, sems.take()) for j in range(2)]
     own = []
     for j in range(2):
         own.append(pltpu.make_async_copy(l_ref.at[j], lraw.at[0, j, pl.ds(0, ROWS), :], local.at[2 * j]))
-        own.append(pltpu.make_async_copy(t_ref.at[j], traw.at[c, j, pl.ds(0, ROWS), :], local.at[2 * j + 1]))
+        own.append(pltpu.make_async_copy(t_halves.at[j], traw.at[c, j, :, pl.ds(0, 120), :], local.at[2 * j + 1]))
 
     hop_l = [
         remote_sized(
@@ -327,7 +325,7 @@
             lraw[part, j, ROWS:PAD, :] = jnp.zeros((PAD - ROWS, V), F32)
     for part in range(4):
         for j in range(2):
-            traw[part, j, ROWS:PAD, :] = jnp.zeros((PAD - ROWS, V), F32)
+            traw[part, j, :, 120:128, :] = jnp.zeros((2, 8, V), F32)
 
     @pl.when(jnp.logical_not(col_big(z)))
     def _():
@@ -338,73 +336,112 @@
     acc[...] = jnp.zeros_like(acc)
     gram[...] = jnp.zeros_like(gram)
 
-    def halves(j, first, n, blocks, parts_l, parts_t):
-        cols = pl.ds(first, n)
-        for part in parts_l:
-
-            @pl.loop(0, PAD // 32)
-            def _(b, part=part):
-                at = pl.multiple_of(b * 32, 32)
-                hi, lo = split(lraw[part, j, pl.ds(at, 32), cols])
-                rows = pl.ds(part * PAD + at, 32)
-                lcat[rows, 0:n] = hi
-                lcat[rows, n : 2 * n] = lo
-                lcat[rows, 2 * n : 3 * n] = hi
-
-        for slot in parts_t:
-
-            @pl.loop(0, 4)
-            def _(b, slot=slot):
-                at = pl.multiple_of(b * 32, 32)
-                hi, lo = split(traw[slot // 2, j, pl.ds(120 * (slot % 2) + at, 32), cols])
-                rows = pl.ds(slot * 128 + at, 32)
-                tcat[rows, 0:n] = hi
-                tcat[rows, n : 2 * n] = hi
-                tcat[rows, 2 * n : 3 * n] = lo
-
-        for n_range, m in blocks:
-
-            @pl.loop(*n_range)
-            def _(b, m=m):
-                r = dot_nt(lcat[m * 256 : (m + 1) * 256, 0 : 3 * n], tcat[pl.ds(pl.multiple_of(b * 256, 256), 256), 0 : 3 * n])
-                rows = slice(m * 256, (m + 1) * 256)
-                acc[b // 2, 2 * (b % 2), rows, :] += r[:, :128]
-                acc[b // 2, 2 * (b % 2) + 1, rows, :] += r[:, 128:]
-
-    def lo(h):
-        return pl.ds(256 * h, 128)
-
-    def hi_of(h, q):
-        return pl.ds(pl.multiple_of(256 * h + 128 + 32 * q, 32), 32)
-
-    early, late, second = [], ([], []), ({}, {})
+    def split_lanes(cut, lanes):
+        j, first, n = cut
+
+        @pl.loop(lanes[0] // 32, lanes[1] // 32)
+        def _(b):
+            at = pl.multiple_of(b * 32, 32)
+            hi, lo = split(lraw[b // 8, j, pl.ds(pl.multiple_of((b % 8) * 32, 32), 32), pl.ds(first, n)])
+            rows = pl.ds(at, 32)
+            lcat[rows, 0:n] = hi
+            lcat[rows, n : 2 * n] = lo
+            lcat[rows, 2 * n : 3 * n] = hi
+
+    def split_rows(cut, block, half):
+        j, first, n = cut
+        y_of, core = lax.div(block, 2), lax.rem(block, 2)
+
+        @pl.loop(0, 4)
+        def _(b):
+            at = pl.multiple_of((b % 2) * 32, 32)
+            hi, lo = split(traw[block, j, b // 2, pl.ds(64 * half + at, 32), pl.ds(first, n)])
+            rows = pl.ds(pl.multiple_of(y_of * 512 + half * 256 + core * 128 + b * 32, 32), 32)
+            tcat[rows, 0:n] = hi
+            tcat[rows, n : 2 * n] = hi
+            tcat[rows, 2 * n : 3 * n] = lo
+
+    def multiply(cut, y_of, half, lanes, core=None):
+        n = cut[2]
+        at = y_of * 512 + half * 256
+        span = pl.ds(at, 256) if core is None else pl.ds(pl.multiple_of(at + core * 128, 128), 128)
+        for lane in range(*lanes, 128 if lanes[1] - lanes[0] == 128 else 256):
+            wide = min(256, lanes[1] - lane)
+            r = dot_nt(tcat[span, 0 : 3 * n], lcat[lane : lane + wide, 0 : 3 * n])
+            if core is None:
+                acc[y_of, half, :, :, :, lane : lane + wide] += r.reshape(4, 2, 32, wide)
+            else:
+                acc[y_of, half, pl.ds(2 * core, 2), :, :, lane : lane + wide] += r.reshape(2, 2, 32, wide)
+
+    def part_of(q):
+        return pl.ds(pl.multiple_of(8 * q, 8), 8)
+
+    firsts, second = {0: ([], []), 1: ([], []), 2: ([], [])}, ({}, {})
+    pieces = (
+        (0, 0, None, 0, 256),
+        (1, 0, None, 256, 128), (1, 1, 0, 0, 384),
+        (2, 0, None, 384, 128), (2, 1, 0, 384, 128), (2, 1, 1, 0, 512),
+    )
+    for when, b, half, lane, wide in pieces:
+        lanes = pl.ds(lane, wide)
+        for d in (1, 3, 2):
+            qx, qz = ring(x + d), ring(z + d)
+
+            def src_z(b=b, half=half, lanes=lanes, qz=qz):
+                return acc.at[b, :, qz, 0, :, lanes] if half is None else acc.at[b, half, qz, 0, :, lanes]
+
+            def dst_z(b=b, half=half, lanes=lanes, d=d):
+                return rz1.at[d - 1, b, :, :, lanes] if half is None else rz1.at[d - 1, b, half, :, lanes]
+
+            def src_x(b=b, half=half, lanes=lanes, qx=qx):
+                return acc.at[b, :, :, 1, part_of(qx), lanes] if half is None else acc.at[b, half, :, 1, part_of(qx), lanes]
+
+            def dst_x(b=b, half=half, lanes=lanes, d=d):
+                return rx1.at[d - 1, b, :, :, :, lanes] if half is None else rx1.at[d - 1, b, half, :, :, lanes]
+
+            firsts[when][b].append(remote(src_z, dst_z, at_z(d), sems.take()))
+            firsts[when][b].append(remote(src_x, dst_x, at_x(d), sems.take()))
     for d in (1, 3, 2):
         qx, qz = ring(x + d), ring(z + d)
-        early.append(remote(lambda qz=qz: acc.at[0, qz, lo(0), :], lambda d=d: rz1.at[d - 1, 0, 0], at_z(d), sems.take()))
-        early.append(remote(lambda qx=qx: acc.at[0, :, hi_of(0, qx), :], lambda d=d: rx1.at[d - 1, 0, 0], at_x(d), sems.take()))
-        late[0].append(remote(lambda qz=qz: acc.at[1, qz, lo(0), :], lambda d=d: rz1.at[d - 1, 0, 1], at_z(d), sems.take()))
-        late[0].append(remote(lambda qx=qx: acc.at[1, :, hi_of(0, qx), :], lambda d=d: rx1.at[d - 1, 0, 1], at_x(d), sems.take()))
-        late[1].append(remote(lambda qz=qz: acc.at[:, qz, lo(1), :], lambda d=d: rz1.at[d - 1, 1], at_z(d), sems.take()))
-        late[1].append(remote(lambda qx=qx: acc.at[:, :, hi_of(1, qx), :], lambda d=d: rx1.at[d - 1, 1], at_x(d), sems.take()))
-        for h in range(2):
-            second[h]["z", d] = remote(lambda qx=qx, h=h: sz.at[h, :, pl.ds(pl.multiple_of(32 * qx, 32), 32), :], lambda d=d, h=h: rz2.at[d - 1, h], at_x(d), sems.take())
-            second[h]["x", d] = remote(lambda qz=qz, h=h: sx.at[h, :, qz], lambda d=d, h=h: rx2.at[d - 1, h], at_z(d), sems.take())
+        for b in range(2):
+            second[b]["z", d] = remote(lambda qx=qx, b=b: sz.at[b, :, part_of(qx), :], lambda d=d, b=b: rz2.at[d - 1, b], at_x(d), sems.take())
+            second[b]["x", d] = remote(lambda qz=qz, b=b: sx.at[b, :, qz], lambda d=d, b=b: rx2.at[d - 1, b], at_z(d), sems.take())
 
     for copy in own:
         copy.wait()
-    for k, (j, first, n) in enumerate(OWN_CUTS):
+    for k, one in enumerate(WIDE):
+        split_lanes(one, (0, 256))
         if k % 3 == 0:
-            core_amps[j].wait_recv()
-        halves(j, first, n, [((0, 2), 0)], (0,), range(4))
-    for copy in early:
-        copy.start()
+            core_amps[one[0]].wait_recv()
+        for half in range(2):
+            pl.loop(0, 2)(lambda block, half=half: split_rows(one, block, half))
+            multiply(one, 0, half, (0, 256))
     for i in range(STEPS):
+        now, one = CUTS[i]
+        fresh = (256 + 128 * now, 384 + 128 * now)
+        split_lanes(one, (0, 256 + 128 * now))
+        for half in range(2):
+            pl.loop(0, 2 + 2 * (half < now))(lambda block, half=half: split_rows(one, block, half))
         y_amps[i].wait_recv()
         forward[i].start()
+        split_rows(one, 2 + c, now)
         y_lambda[i].wait_recv()
+        split_lanes(one, fresh)
+        for half in range(2):
+            multiply(one, 0, half, fresh)
+        if i == STEPS - 1:
+            for copy in firsts[2][0]:
+                copy.start()
+        if now == 1:
+            multiply(one, 1, 0, fresh)
+        multiply(one, 1, now, (0, fresh[1]), c)
         forward[i].wait_recv()
-        halves(*CUTS[i], [((0, 4), 1), ((2, 4), 0)], (0, 1), range(8))
-        if i == 2:
+        split_rows(one, 3 - c, now)
+        multiply(one, 1, now, (0, fresh[1]), 1 - c)
+        if i == STEPS - 3:
+            for copy in firsts[0][0] + firsts[1][0] + firsts[1][1]:
+                copy.start()
+        if i == 5:
             for d in (1, 3, 2):
                 got_l[d - 1].wait_recv()
                 for e in (1, 3, 2):
@@ -420,7 +457,7 @@
                 keep_t[d].start()
                 for copy in hold[d]:
                     copy.start()
-    for copy in late[0] + late[1]:
+    for copy in firsts[2][1]:
         copy.start()
 
     for d in range(4):
@@ -466,33 +503,35 @@
 
     over_group = share(ig, virt, at_group, inter)
 
-    def sum_first(h):
-        for copy in (early if h == 0 else []) + late[h]:
+    def sum_first(b):
+        for when in firsts.values():
+            for copy in when[b]:
+                copy.wait_recv()
+        for half in range(2):
+            sz[b, half] = (acc[b, half, z, 0] + rz1[0, b, half]) + (rz1[1, b, half] + rz1[2, b, half])
+        for d in (1, 3, 2):
+            second[b]["z", d].start()
+        for half in range(2):
+            sx[b, half] = (acc[b, half, :, 1, part_of(x), :] + rx1[0, b, half]) + (rx1[1, b, half] + rx1[2, b, half])
+        for d in (1, 3, 2):
+            second[b]["x", d].start()
+
+    lasts = []
+
+    def sum_second(b):
+        for copy in second[b].values():
             copy.wait_recv()
-        for b in range(2):
-            sz[h, b] = (acc[b, z, lo(h), :] + rz1[0, h, b]) + (rz1[1, h, b] + rz1[2, h, b])
-        for d in (1, 3, 2):
-            second[h]["z", d].start()
-        for b in range(2):
-            for q in range(4):
-                sx[h, b, q] = (acc[b, q, hi_of(h, x), :] + rx1[0, h, b, q]) + (rx1[1, h, b, q] + rx1[2, h, b, q])
-        for d in (1, 3, 2):
-            second[h]["x", d].start()
-
-    lasts = []
-
-    def sum_second(h):
-        for copy in second[h].values():
-            copy.wait_recv()
-        mine = pl.ds(pl.multiple_of(32 * x, 32), 32)
-        for b, q in ((0, y), (1, y_t)):
-            done[h, b, 0] = (sz[h, b, mine, :] + rz2[0, h, b]) + (rz2[1, h, b] + rz2[2, h, b])
-            done[h, b, 1] = (sx[h, b, z] + rx2[0, h, b]) + (rx2[1, h, b] + rx2[2, h, b])
+        for half in range(2):
+            done[b, half, 0] = (sz[b, half, part_of(x), :] + rz2[0, b, half]) + (rz2[1, b, half] + rz2[2, b, half])
+            done[b, half, 1] = (sx[b, half, z] + rx2[0, b, half]) + (rx2[1, b, half] + rx2[2, b, half])
+        q = (y, y_t)[b]
+        for h in range(2):
             s = sems.take()[0]
-            make = lambda b=b, q=q, s=s: pltpu.make_async_remote_copy(src_ref=done.at[h, b], dst_ref=fin.at[:, x], send_sem=s, recv_sem=recv.at[N_SEMS - 4 + x], device_id=dev(q, z, (y, y_l)[h], c), device_id_type=MESH)
+            block = lambda h=h: done.at[b, :, :, :, pl.ds(256 * h, 256)]
+            make = lambda h=h, s=s, block=block: pltpu.make_async_remote_copy(src_ref=block(), dst_ref=fin.at[:, :, x], send_sem=s, recv_sem=recv.at[N_SEMS - 4 + x], device_id=dev(q, z, (y, y_l)[h], c), device_id_type=MESH)
             if h == 0:
                 go = Copy((q != x, make))
-                stay = Copy((q == x, lambda b=b: pltpu.make_async_copy(done.at[0, b], fin.at[:, x], local.at[12])))
+                stay = Copy((q == x, lambda block=block: pltpu.make_async_copy(block(), fin.at[:, :, x], local.at[12])))
                 stay.start()
             else:
                 go, stay = Copy((None, make)), Copy()
@@ -514,45 +553,45 @@
     same_k = lax.dot_general(kind, kind, (((0,), (0,)), ((), ())), preferred_element_type=F32)
     highest = lax.Precision.HIGHEST
     outer = lax.dot_general(one_hot, same_k * matrix, (((1,), (0,)), ((), ())), precision=highest, preferred_element_type=F32)
-    occ_ref[...] = -lax.dot_general(outer, one_hot, NT, precision=highest, preferred_element_type=F32)
+    occ_ref[...] = -lax.dot_general(outer, one_hot, NT, precision=highest, preferred_element_type=F32)[:OCC]
 
     for go, stay in lasts:
         stay.wait()
     in_plane = (x == y) | (x == y_t)
     for q in range(4):
-        came = Copy((jnp.logical_not(in_plane & (x == q)), lambda q=q: pltpu.make_async_remote_copy(src_ref=done.at[0, 0], dst_ref=fin.at[:, q], send_sem=send.at[0], recv_sem=recv.at[N_SEMS - 4 + q], device_id=to_l, device_id_type=MESH)))
+        came = Copy((jnp.logical_not(in_plane & (x == q)), lambda q=q: pltpu.make_async_remote_copy(src_ref=fin.at[:, :, q], dst_ref=fin.at[:, :, q], send_sem=send.at[0], recv_sem=recv.at[N_SEMS - 4 + q], device_id=to_l, device_id_type=MESH)))
         came.wait_recv()
 
     sent = y_lambda + y_amps + forward + core_amps + hop_l + hop_t + list(second_l.values()) + list(second_t.values())
     for group in (hop_s, more_l, more_t):
         sent += list(group.values())
-    sent += early + late[0] + late[1] + list(second[0].values()) + list(second[1].values()) + [go for go, _ in lasts] + over_group + over_plane
+    sent += [copy for when in firsts.values() for one in when for copy in one] + list(second[0].values()) + list(second[1].values()) + [go for go, _ in lasts] + over_group + over_plane
     for copy in sent:
         copy.wait_send()
 
 
 def finish(fin_ref, occ_in, virt_ref, occ_ref):
-    virt_ref[...] = fin_ref[...].reshape(256, 128)[:ROWS, :120]
-    occ_ref[...] = occ_in[:OCC, :OCC]
+    virt_ref[...] = fin_ref[...].reshape(128, 256).T[:ROWS, :120]
+    occ_ref[...] = occ_in[:, :OCC]
 
 
 def shards(lambda_blocks, amplitudes, pair_list):
     vmem = lambda shape, dtype=F32: pltpu.VMEM(shape, dtype)
     fin, occ = pl.pallas_call(
         kernel,
-        out_shape=(jax.ShapeDtypeStruct((2, 4, 32, 128), F32), jax.ShapeDtypeStruct((256, 256), F32)),
-        in_specs=[pl.BlockSpec(memory_space=pl.ANY)] * 3,
-        out_specs=(pl.BlockSpec(memory_space=pltpu.VMEM),) * 2,
+        out_shape=(jax.ShapeDtypeStruct((2, 2, 4, 8, 256), F32), jax.ShapeDtypeStruct((OCC, 256), F32)),
+        in_specs=[pl.BlockSpec(memory_space=pl.ANY)] * 4,
+        out_specs=(pl.BlockSpec(memory_space=pl.ANY), pl.BlockSpec(memory_space=pltpu.VMEM)),
         scratch_shapes=[
-            vmem((2, 2, PAD, V)), vmem((4, 2, PAD, V)), vmem((512, 3 * KC), BF16), vmem((1024, 3 * KC), BF16), vmem((2, 4, 512, 128)),
+            vmem((2, 2, PAD, V)), vmem((4, 2, 2, 128, V)), vmem((512, 3 * KC), BF16), vmem((1024, 3 * KC), BF16), vmem((2, 2, 4, 2, 32, 512)),
             vmem((3, 2, 64, V)), vmem((3, 2, ROWS, 512)), vmem((4, 4, 2, 64, 512)), vmem((4, 4, 2, 64, 512)), vmem((256, 256)),
-            vmem((3, 2, 2, 128, 128)), vmem((3, 2, 2, 4, 32, 128)), vmem((3, 2, 2, 32, 128)), vmem((3, 2, 2, 32, 128)),
-            vmem((2, 2, 128, 128)), vmem((2, 2, 4, 32, 128)), vmem((2, 2, 2, 32, 128)), vmem((8, 8, 128)), vmem((16, 8, 128)), vmem((2, NP), jnp.int32),
+            vmem((3, 2, 2, 32, 512)), vmem((3, 2, 2, 4, 8, 512)), vmem((3, 2, 2, 8, 512)), vmem((3, 2, 2, 8, 512)),
+            vmem((2, 2, 32, 512)), vmem((2, 2, 4, 8, 512)), vmem((2, 2, 2, 8, 512)), vmem((8, 8, 128)), vmem((16, 8, 128)), vmem((2, NP), jnp.int32),
             pltpu.SemaphoreType.DMA((N_SEMS,)), pltpu.SemaphoreType.DMA((N_SEMS,)), pltpu.SemaphoreType.DMA((22,)),
         ],
         compiler_params=pltpu.CompilerParams(collective_id=0, has_side_effects=True, vmem_limit_bytes=60 * 2**20),
         cost_estimate=pl.CostEstimate(flops=12_000_000_000, bytes_accessed=8_000_000, transcendentals=0),
-    )(lambda_blocks, amplitudes, pair_list.T)
+    )(lambda_blocks, amplitudes, amplitudes.reshape(2, 2, 120, V), pair_list.T)
     return pl.pallas_call(
         finish,
         out_shape=(jax.ShapeDtypeStruct((ROWS, 120), F32), jax.ShapeDtypeStruct((OCC, OCC), F32)),

time: 119 us -> 117 us (0.983); the launches traced: 118 us -> 117 us
  no operation moved by 1% of the time
where the time goes in v3:
time: 117 us
  Pallas kernels  116 us (99%)
    pallas_call x1, Pallas kernels, shards(): pl.pallas_call(kernel, out_shape=(jax.ShapeDtypeStruct((2, 2, 4, 8, 256),...  115 us

profile of v3, /device:TPU:16, one launch (start us, length us, event | category | flops | bytes accessed | tf_op | source)
XLA Modules:
  0.0 116.9 jit_solution(11628319122107147903)
XLA Ops:
  0.6 114.5 %shard_map.50 = (f32[2,2,4,8,256]{4,3,2,1,0:T(8,128)}, f32[200,256]{1,0:T(8,128)}) custom-call(f32[2,240,1920]{2,1,0:T(8,128)} %l_ref.1, f32[2,240,1920]{2,1,0:T(8,128)} %t_ref.1, f32[2,2,120,1920]{3,2,1,0:T(8,128)} %bitcast.2, s32[2,32]{1,0:T(2,128)} %bitcast.3), custom_call_target="tpu_custom_call" | custom-call | flops 12000000000 | bytes 8000000 | tf_op jit(solution)/shard_map/pallas_call | solution.py:580
  115.1 1.7 %shard_map.51 = (f32[240,120]{1,0:T(8,128)}, f32[200,200]{1,0:T(8,128)}) custom-call(f32[2,2,4,8,256]{4,3,2,1,0:T(8,128)} %get-tuple-element.4.fin_ref, f32[200,256]{1,0:T(8,128)} %get-tuple-element.5.occ_in), custom_call_target="tpu_custom_call" | custom-call | tf_op jit(solution)/shard_map/pallas_call | solution.py:595

commit v4 on v3

--- a/solution.py
+++ b/solution.py
@@ -68,7 +68,7 @@
     return lax.dot_general(a, b, NT, preferred_element_type=F32)
 
 
-N_SEMS = 192
+N_SEMS = 224
 
 
 def kernel(
@@ -376,11 +376,12 @@
     def part_of(q):
         return pl.ds(pl.multiple_of(8 * q, 8), 8)
 
-    firsts, second = {0: ([], []), 1: ([], []), 2: ([], [])}, ({}, {})
+    firsts, second = {0: ([], []), 1: ([], []), 2: ([], [])}, {}
+    groups = {(b, h): [] for b in range(2) for h in range(2)}
     pieces = (
         (0, 0, None, 0, 256),
-        (1, 0, None, 256, 128), (1, 1, 0, 0, 384),
-        (2, 0, None, 384, 128), (2, 1, 0, 384, 128), (2, 1, 1, 0, 512),
+        (1, 0, None, 256, 128), (1, 1, 0, 0, 256), (1, 1, 0, 256, 128),
+        (2, 0, None, 384, 128), (2, 1, 1, 0, 256), (2, 1, 0, 384, 128), (2, 1, 1, 256, 256),
     )
     for when, b, half, lane, wide in pieces:
         lanes = pl.ds(lane, wide)
@@ -399,13 +400,15 @@
             def dst_x(b=b, half=half, lanes=lanes, d=d):
                 return rx1.at[d - 1, b, :, :, :, lanes] if half is None else rx1.at[d - 1, b, half, :, :, lanes]
 
-            firsts[when][b].append(remote(src_z, dst_z, at_z(d), sems.take()))
-            firsts[when][b].append(remote(src_x, dst_x, at_x(d), sems.take()))
+            both = [remote(src_z, dst_z, at_z(d), sems.take()), remote(src_x, dst_x, at_x(d), sems.take())]
+            firsts[when][b].extend(both)
+            groups[b, lane // 256].extend(both)
     for d in (1, 3, 2):
         qx, qz = ring(x + d), ring(z + d)
-        for b in range(2):
-            second[b]["z", d] = remote(lambda qx=qx, b=b: sz.at[b, :, part_of(qx), :], lambda d=d, b=b: rz2.at[d - 1, b], at_x(d), sems.take())
-            second[b]["x", d] = remote(lambda qz=qz, b=b: sx.at[b, :, qz], lambda d=d, b=b: rx2.at[d - 1, b], at_z(d), sems.take())
+        for b, h in groups:
+            lanes = pl.ds(256 * h, 256)
+            second[b, h, "z", d] = remote(lambda qx=qx, b=b, k=lanes: sz.at[b, :, part_of(qx), k], lambda d=d, b=b, k=lanes: rz2.at[d - 1, b, :, :, k], at_x(d), sems.take())
+            second[b, h, "x", d] = remote(lambda qz=qz, b=b, k=lanes: sx.at[b, :, qz, :, k], lambda d=d, b=b, k=lanes: rx2.at[d - 1, b, :, :, k], at_z(d), sems.take())
 
     for copy in own:
         copy.wait()
@@ -503,46 +506,51 @@
 
     over_group = share(ig, virt, at_group, inter)
 
-    def sum_first(b):
-        for when in firsts.values():
-            for copy in when[b]:
-                copy.wait_recv()
+    def sum_first(b, h):
+        for copy in groups[b, h]:
+            copy.wait_recv()
+        k = pl.ds(256 * h, 256)
         for half in range(2):
-            sz[b, half] = (acc[b, half, z, 0] + rz1[0, b, half]) + (rz1[1, b, half] + rz1[2, b, half])
+            sz[b, half, :, k] = (acc[b, half, z, 0, :, k] + rz1[0, b, half, :, k]) + (rz1[1, b, half, :, k] + rz1[2, b, half, :, k])
         for d in (1, 3, 2):
-            second[b]["z", d].start()
+            second[b, h, "z", d].start()
         for half in range(2):
-            sx[b, half] = (acc[b, half, :, 1, part_of(x), :] + rx1[0, b, half]) + (rx1[1, b, half] + rx1[2, b, half])
+            sx[b, half, :, :, k] = (acc[b, half, :, 1, part_of(x), k] + rx1[0, b, half, :, :, k]) + (rx1[1, b, half, :, :, k] + rx1[2, b, half, :, :, k])
         for d in (1, 3, 2):
-            second[b]["x", d].start()
+            second[b, h, "x", d].start()
 
     lasts = []
 
-    def sum_second(b):
-        for copy in second[b].values():
-            copy.wait_recv()
+    def sum_second(b, h):
+        for d in (1, 2, 3):
+            second[b, h, "z", d].wait_recv()
+            second[b, h, "x", d].wait_recv()
+        k = pl.ds(256 * h, 256)
         for half in range(2):
-            done[b, half, 0] = (sz[b, half, part_of(x), :] + rz2[0, b, half]) + (rz2[1, b, half] + rz2[2, b, half])
-            done[b, half, 1] = (sx[b, half, z] + rx2[0, b, half]) + (rx2[1, b, half] + rx2[2, b, half])
+            done[b, half, 0, :, k] = (sz[b, half, part_of(x), k] + rz2[0, b, half, :, k]) + (rz2[1, b, half, :, k] + rz2[2, b, half, :, k])
+            done[b, half, 1, :, k] = (sx[b, half, z, :, k] + rx2[0, b, half, :, k]) + (rx2[1, b, half, :, k] + rx2[2, b, half, :, k])
         q = (y, y_t)[b]
-        for h in range(2):
-            s = sems.take()[0]
-            block = lambda h=h: done.at[b, :, :, :, pl.ds(256 * h, 256)]
-            make = lambda h=h, s=s, block=block: pltpu.make_async_remote_copy(src_ref=block(), dst_ref=fin.at[:, :, x], send_sem=s, recv_sem=recv.at[N_SEMS - 4 + x], device_id=dev(q, z, (y, y_l)[h], c), device_id_type=MESH)
-            if h == 0:
-                go = Copy((q != x, make))
-                stay = Copy((q == x, lambda block=block: pltpu.make_async_copy(block(), fin.at[:, :, x], local.at[12])))
-                stay.start()
-            else:
-                go, stay = Copy((None, make)), Copy()
-            go.start()
-            lasts.append((go, stay))
-
-    sum_first(0)
+        s = sems.take()[0]
+        block = lambda: done.at[b, :, :, :, k]
+        go = lambda: pltpu.make_async_remote_copy(src_ref=block(), dst_ref=fin.at[:, :, x], send_sem=s, recv_sem=recv.at[N_SEMS - 4 + x], device_id=dev(q, z, (y, y_l)[h], c), device_id_type=MESH)
+        if h == 0:
+            go = Copy((q != x, go))
+            stay = Copy((q == x, lambda: pltpu.make_async_copy(block(), fin.at[:, :, x], local.at[12])))
+            stay.start()
+        else:
+            go, stay = Copy((None, go)), Copy()
+        go.start()
+        lasts.append((go, stay))
+
+    sum_first(0, 0)
+    sum_first(0, 1)
+    sum_first(1, 0)
+    sum_first(1, 1)
     over_plane = share(ip, pair, at_plane, total(ig, over_group, 8))
-    sum_first(1)
-    sum_second(0)
-    sum_second(1)
+    sum_second(0, 0)
+    sum_second(0, 1)
+    sum_second(1, 0)
+    sum_second(1, 1)
 
     every = total(ip, over_plane, 16)
     matrix = jnp.concatenate([every[:, 32 * k : 32 * k + 32] for k in range(4)], axis=0)
@@ -565,7 +573,7 @@
     sent = y_lambda + y_amps + forward + core_amps + hop_l + hop_t + list(second_l.values()) + list(second_t.values())
     for group in (hop_s, more_l, more_t):
         sent += list(group.values())
-    sent += [copy for when in firsts.values() for one in when for copy in one] + list(second[0].values()) + list(second[1].values()) + [go for go, _ in lasts] + over_group + over_plane
+    sent += [copy for when in firsts.values() for one in when for copy in one] + list(second.values()) + [go for go, _ in lasts] + over_group + over_plane
     for copy in sent:
         copy.wait_send()
 

time: 117 us -> 117 us (level)
  no operation moved by 1% of the time
where the time goes in v4:
time: 117 us
  Pallas kernels  116 us (99%)
    pallas_call x1, Pallas kernels, shards(): pl.pallas_call(kernel, out_shape=(jax.ShapeDtypeStruct((2, 2, 4, 8, 256),...  114 us

profile of v4, /device:TPU:16, one launch (start us, length us, event | category | flops | bytes accessed | tf_op | source)
XLA Modules:
  0.0 116.8 jit_solution(5402994700150648575)
XLA Ops:
  0.6 114.4 %shard_map.50 = (f32[2,2,4,8,256]{4,3,2,1,0:T(8,128)}, f32[200,256]{1,0:T(8,128)}) custom-call(f32[2,240,1920]{2,1,0:T(8,128)} %l_ref.1, f32[2,240,1920]{2,1,0:T(8,128)} %t_ref.1, f32[2,2,120,1920]{3,2,1,0:T(8,128)} %bitcast.2, s32[2,32]{1,0:T(2,128)} %bitcast.3), custom_call_target="tpu_custom_call" | custom-call | flops 12000000000 | bytes 8000000 | tf_op jit(solution)/shard_map/pallas_call | solution.py:588
  115.0 1.7 %shard_map.51 = (f32[240,120]{1,0:T(8,128)}, f32[200,200]{1,0:T(8,128)}) custom-call(f32[2,2,4,8,256]{4,3,2,1,0:T(8,128)} %get-tuple-element.4.fin_ref, f32[200,256]{1,0:T(8,128)} %get-tuple-element.5.occ_in), custom_call_target="tpu_custom_call" | custom-call | tf_op jit(solution)/shard_map/pallas_call | solution.py:603
